TPU v7x, 128 devices: a whole 4x4x4 slice. The times are simulated.
128 devices in a mesh: elem: 32 (over z, y, core), span: 4 (over x).
Axes of the slice: x: 4, y: 4, z: 4, core: 2. Of those that a mesh axis runs over, the one named last changes fastest.
Arguments:
- state: float32 [512, 32, 128], P('elem', 'span'), may hold values from -6 to 6
- assignment: int32 [512, 32], P('elem', 'span'), may hold values from 0 to 32767, as said below
- surface: bfloat16 [32768, 16], P(('elem', 'span')), may hold values from -6 to 6
- w_state: bfloat16 [4, 2048], replicated, may hold values from -3 to 3
- w_surf: bfloat16 [16, 2048], replicated, may hold values from -1.5 to 1.5
- w_hidden: bfloat16 [512, 2048], replicated, may hold values from -0.25 to 0.25
- bias: float32 [2048], replicated, may hold values from -3 to 3
- w_out: bfloat16 [512, 4], replicated, may hold values from -0.25 to 0.25
Outputs:
- new_state: float32 [512, 32, 128], P('elem', 'span')
Inputs may be any that keep to these rules, and one draw needn't show every extreme that they name: `assignment`: each value is a physics device index (elem index times the span axis size plus span index) times 256 plus a slot below 256. No two columns share a value. The columns of one device take at most 2 slots of any one physics device, and every device takes 2 slots of some physics device; some physics device has all 256 slots taken.
All inputs are finite; a program needn't handle non-finite values.
Results may differ from a plain program's by a relative error of at most 0.0017.
Values may be sent and summed in bfloat16 or wider, within the bound.
No kernel may reach another device: no remote copies, remote signals or barrier semaphores. Data moves between devices by JAX's collectives and lax.ppermute only.
A program may use at most 64 MiB of HBM per device.

v0:
```python
import math

import jax
import jax.numpy as jnp
import numpy as np
from jax import lax
from jax.sharding import PartitionSpec as P

NP = 4
NV = 4
SUBSTEPS = 2


courant = 0.05


def with_halo(value, sides, width):
    for axis, dim in sides:
        size, length = (lax.axis_size(axis), value.shape[dim])
        up = [(i, (i + 1) % size) for i in range(size)]
        down = [(j, i) for i, j in up]
        last = lax.slice_in_dim(value, length - width, length, axis=dim)
        leading = lax.slice_in_dim(value, 0, width, axis=dim)
        before = lax.ppermute(last, axis, up)
        after = lax.ppermute(leading, axis, down)
        value = jnp.concatenate([before, value, after], axis=dim)
    return value


def gll_table():
    nodes = np.array([-1.0, -1.0 / math.sqrt(5.0), 1.0 / math.sqrt(5.0), 1.0])
    width = nodes.shape[0]
    table = np.zeros((width, width))
    for row in range(width):
        for column in range(width):
            if row != column:
                upper = np.prod(
                    [nodes[row] - nodes[other] for other in range(width) if other != row]
                )
                lower = np.prod(
                    [nodes[column] - nodes[other] for other in range(width) if other != column]
                )
                table[row, column] = upper / (lower * (nodes[row] - nodes[column]))
            else:
                table[row, row] = sum(
                    (1.0 / (nodes[row] - nodes[other]) for other in range(width) if other != row)
                )
    return table


def derivative(grid, position):
    table = gll_table()
    pieces = []
    for row in range(NP):
        total = None
        for column in range(NP):
            term = float(table[row, column]) * lax.index_in_dim(
                grid, column, position, keepdims=False
            )
            total = term if total is None else total + term
        pieces.append(total)
    return jnp.stack(pieces, axis=position)


def advect(field):
    rows, columns, channels = field.shape
    grid = field.reshape(rows // NP, NP, columns // NP, NP, channels // NV, NV)
    along_x = derivative(grid, 1)
    along_y = derivative(grid, 3)
    wind_x = grid[..., 0:1]
    wind_y = grid[..., 1:2]
    moved = grid - courant * (wind_x * along_x + wind_y * along_y)
    return moved.reshape(rows, columns, channels)


def average_edges(padded):
    rows = padded.shape[0] - 2
    middle = padded[1:-1]
    position = (jnp.arange(rows) % NP)[:, None, None]
    first = jnp.where(
        position == NP - 1,
        (middle + padded[2:]) * 0.5,
        jnp.where(position == 0, (middle + padded[:-2]) * 0.5, middle),
    )
    columns = first.shape[1] - 2
    centre = first[:, 1:-1]
    place = (jnp.arange(columns) % NP)[None, :, None]
    return jnp.where(
        place == NP - 1,
        (centre + first[:, 2:]) * 0.5,
        jnp.where(place == 0, (centre + first[:, :-2]) * 0.5, centre),
    )


def imitate(columns, surf, w_state, w_surf, w_hidden, bias, w_out):
    rows = columns.shape[0]
    levels = columns.shape[1] // NV
    hidden_size = w_hidden.shape[0]
    base = jnp.dot(surf, w_surf, preferred_element_type=jnp.float32) + bias
    inputs = jnp.transpose(columns.reshape(rows, levels, NV), (1, 0, 2))

    def advance(carry, level_in):
        hidden, cell = carry
        gates = (
            base
            + jnp.dot(level_in, w_state, preferred_element_type=jnp.float32)
            + jnp.dot(hidden, w_hidden, preferred_element_type=jnp.float32)
        )
        inner, forget, candidate, output = jnp.split(gates, 4, axis=1)
        cell = jax.nn.sigmoid(forget) * cell + jax.nn.sigmoid(inner) * jnp.tanh(candidate)
        hidden = (jax.nn.sigmoid(output) * jnp.tanh(cell)).astype(jnp.bfloat16)
        return ((hidden, cell), jnp.dot(hidden, w_out, preferred_element_type=jnp.float32))

    start = (
        jnp.zeros((rows, hidden_size), jnp.bfloat16),
        jnp.zeros((rows, hidden_size), jnp.float32),
    )
    _, outputs = lax.scan(advance, start, inputs)
    return jnp.transpose(outputs, (1, 0, 2)).reshape(rows, levels * NV).astype(jnp.bfloat16)


def shards(state, assignment, surface, w_state, w_surf, w_hidden, bias, w_out):
    node_rows, node_cols, channels = state.shape
    field = state
    for substep in range(SUBSTEPS):
        field = advect(field)
        padded = with_halo(field, (("elem", 0), ("span", 1)), 1)
        field = average_edges(padded)
    elem_count = lax.axis_size("elem")
    span_count = lax.axis_size("span")
    devices = elem_count * span_count
    columns_here = node_rows * node_cols
    capacity = 2 * columns_here // devices
    slot_count = surface.shape[0]
    slots = assignment.reshape(columns_here)
    owners = slots // slot_count
    places = slots % slot_count
    matches = (owners[:, None] == jnp.arange(devices, dtype=jnp.int32)[None, :]).astype(jnp.int32)
    earlier = jnp.cumsum(matches, axis=0) - matches
    ranks = jnp.sum(earlier * matches, axis=1)
    positions = owners * capacity + ranks
    columns = field.reshape(columns_here, channels)
    requests = jnp.full((devices * capacity,), slot_count, jnp.int32).at[positions].set(places)
    outgoing = (
        jnp.zeros((devices * capacity, channels), jnp.bfloat16)
        .at[positions]
        .set(columns.astype(jnp.bfloat16))
    )
    arrived, arrived_ids = (
        lax.all_to_all(
            outgoing.reshape(devices, capacity, channels),
            ("elem", "span"),
            split_axis=0,
            concat_axis=0,
            tiled=True,
        ),
        lax.all_to_all(
            requests.reshape(devices, capacity),
            ("elem", "span"),
            split_axis=0,
            concat_axis=0,
            tiled=True,
        ),
    )
    flat_ids = arrived_ids.reshape(devices * capacity)
    packed = (
        jnp.zeros((slot_count, channels), jnp.bfloat16)
        .at[flat_ids]
        .set(arrived.reshape(devices * capacity, channels), mode="drop")
    )
    tendency = imitate(packed, surface, w_state, w_surf, w_hidden, bias, w_out)
    replies = jnp.take(tendency, jnp.minimum(flat_ids, slot_count - 1), axis=0)
    returned = lax.all_to_all(
        replies.reshape(devices, capacity, channels),
        ("elem", "span"),
        split_axis=0,
        concat_axis=0,
        tiled=True,
    )
    mine = jnp.take(returned.reshape(devices * capacity, channels), positions, axis=0)
    return field + mine.reshape(node_rows, node_cols, channels).astype(jnp.float32)


def solution(mesh):
    placed = (
        P("elem", "span", None),
        P("elem", "span"),
        P(("elem", "span"), None),
        P(),
        P(),
        P(),
        P(),
        P(),
    )
    return jax.shard_map(
        shards, mesh=mesh, in_specs=placed, out_specs=P("elem", "span", None), check_vma=False
    )
```

profile of v0, /device:TPU:1, one launch (start us, length us, event | category | flops | bytes accessed | tf_op | source)
XLA Modules:
  0.0 277.0 jit_solution(14503400339885575766)
XLA Ops:
  0.0 3.0 %reshape.262 = f32[4,4,2,4,32,4]{5,4,3,2,1,0:T(8,128)S(1)} reshape(f32[16,8,128]{2,1,0:T(8,128)} %param.10) | data formatting | bytes 131072 | tf_op jit(solution)/shard_map/reshape | solution.py:67
  15.9 2.8 collective-permute-start
  21.2 10.6 %all-to-all-start = ((s32[128,1,2]{2,1,0:T(1,128)}), s32[128,1,2]{2,1,0:T(1,128)S(1)}, u32[]{:S(2)}, u32[]{:S(2)}) async-start(s32[128,1,2]{2,1,0:T(1,128)} %bitcast.2), calls=%async_computation | async-start | bytes 131072 | tf_op jit(solution)/shard_map/all_to_all | solution.py:157
  36.7 4.7 %all-to-all-done = s32[128,1,2]{2,1,0:T(1,128)S(1)} async-done(((s32[128,1,2]{2,1,0:T(1,128)}), s32[128,1,2]{2,1,0:T(1,128)S(1)}, u32[]{:S(2)}, u32[]{:S(2)}) %all-to-all-start) | async-done | bytes 1056 | tf_op jit(solution)/shard_map/all_to_all | solution.py:157
  66.6 2.4 collective-permute-start.7
  71.7 11.4 %all-to-all-start.1 = ((bf16[128,2,128]{2,1,0:T(2,128)(2,1)}), bf16[128,2,128]{2,1,0:T(2,128)(2,1)S(1)}, u32[]{:S(2)}, u32[]{:S(2)}) async-start(bf16[128,2,128]{2,1,0:T(2,128)(2,1)} %bitcast.6), calls=%async_computation.1 | async-start | bytes 131072 | tf_op jit(solution)/shard_map/all_to_all | solution.py:150
  83.1 9.7 %all-to-all-done.1 = bf16[128,2,128]{2,1,0:T(2,128)(2,1)S(1)} async-done(((bf16[128,2,128]{2,1,0:T(2,128)(2,1)}), bf16[128,2,128]{2,1,0:T(2,128)(2,1)S(1)}, u32[]{:S(2)}, u32[]{:S(2)}) %all-to-all-start.1) | async-done | bytes 65568 | tf_op jit(solution)/shard_map/all_to_all | solution.py:150
  94.4 165.4 %while.15 = (s32[]{:T(128)}, bf16[256,512]{1,0:T(8,128)(2,1)S(1)}, f32[256,512]{1,0:T(8,128)S(1)}, bf16[32,256,4]{1,2,0:T(4,128)(2,1)S(1)}, bf16[32,256,4]{1,2,0...) while((s32[]{:T(128)}, bf16[256,512]{1,0:T(8,128)(2,1)S(1)}, ...), condition=%wide.region_6.7_spmd.clone, body=%wide.region_5.6_spmd.clone.sunk | while | flops 545259520 | bytes 14444672 | solution.py:118
  96.5 2.3 convolution_add_fusion.6
  106.8 2.3 convolution_add_fusion.6
  112.0 2.3 convolution_add_fusion.6
  117.2 2.3 convolution_add_fusion.6
  122.3 2.3 convolution_add_fusion.6
  127.5 2.3 convolution_add_fusion.6
  132.7 2.3 convolution_add_fusion.6
  137.8 2.3 convolution_add_fusion.6
  143.0 2.3 convolution_add_fusion.6
  148.2 2.3 convolution_add_fusion.6
  153.3 2.3 convolution_add_fusion.6
  158.5 2.3 convolution_add_fusion.6
  163.7 2.3 convolution_add_fusion.6
  168.9 2.3 convolution_add_fusion.6
  174.0 2.3 convolution_add_fusion.6
  179.2 2.3 convolution_add_fusion.6
  184.4 2.3 convolution_add_fusion.6
  189.5 2.3 convolution_add_fusion.6
  205.1 2.3 convolution_add_fusion.6
  220.6 2.3 convolution_add_fusion.6
  236.1 2.3 convolution_add_fusion.6
  251.6 2.3 convolution_add_fusion.6
  261.7 4.3 %all-to-all-start.2 = ((bf16[128,2,128]{2,1,0:T(2,128)(2,1)}), bf16[128,2,128]{2,1,0:T(2,128)(2,1)S(1)}, u32[]{:S(2)}, u32[]{:S(2)}) async-start(bf16[128,2,128]{2,1,0:T(2,128)(2,1)} %broadcast_select_fusion), calls=%async_computation.2 | async-start | bytes 131072 | tf_op jit(solution)/shard_map/all_to_all | solution.py:173
  266.0 9.6 %all-to-all-done.2 = bf16[128,2,128]{2,1,0:T(2,128)(2,1)S(1)} async-done(((bf16[128,2,128]{2,1,0:T(2,128)(2,1)}), bf16[128,2,128]{2,1,0:T(2,128)(2,1)S(1)}, u32[]{:S(2)}, u32[]{:S(2)}) %all-to-all-start.2) | async-done | bytes 65568 | tf_op jit(solution)/shard_map/all_to_all | solution.py:173
  (239 shorter events, 166.4 us)
Async XLA Ops:
  0.0 31.9 %copy-start = (bf16[16,2048]{1,0:T(8,128)(2,1)S(1)}, bf16[16,2048]{1,0:T(8,128)(2,1)}, u32[]{:S(2)}) copy-start(bf16[16,2048]{1,0:T(8,128)(2,1)} %param.14) | copy-start | bytes 196612
  7.5 4.1 %copy-start.7 = (f32[4,4,2,1,32,4]{5,4,3,2,1,0:T(8,128)S(1)}, f32[4,4,2,1,32,4]{5,4,3,2,1,0:T(8,128)}, u32[]{:S(2)}) copy-start(f32[4,4,2,1,32,4]{5,4,3,2,1,0:T(8,128)} %get-tuple-element.118) | copy-start | bytes 49156
  7.5 4.3 %copy-start.5 = (f32[4,1,2,4,32,4]{5,4,3,2,1,0:T(8,128)S(1)}, f32[4,1,2,4,32,4]{5,4,3,2,1,0:T(8,128)}, u32[]{:S(2)}) copy-start(f32[4,1,2,4,32,4]{5,4,3,2,1,0:T(8,128)} %get-tuple-element.119) | copy-start | bytes 49156
  7.5 4.6 %copy-start.3 = (f32[4,1,2,4,32,4]{5,4,3,2,1,0:T(8,128)S(1)}, f32[4,1,2,4,32,4]{5,4,3,2,1,0:T(8,128)}, u32[]{:S(2)}) copy-start(f32[4,1,2,4,32,4]{5,4,3,2,1,0:T(8,128)} %get-tuple-element.122) | copy-start | bytes 49156
  13.4 2.5 copy-start.9
  13.4 5.3 %copy-start.15 = (s32[16,8]{0,1:T(8,128)S(1)}, s32[16,8]{0,1:T(8,128)}, u32[]{:S(2)}) copy-start(s32[16,8]{0,1:T(8,128)} %param.11) | copy-start | bytes 1540
  13.4 18.5 %copy-start.13 = (bf16[256,16]{0,1:T(8,128)(2,1)S(1)}, bf16[256,16]{0,1:T(8,128)(2,1)}, u32[]{:S(2)}) copy-start(bf16[256,16]{0,1:T(8,128)(2,1)} %param.12) | copy-start | bytes 24580
  13.4 18.5 %copy-start.14 = (f32[2048]{0:T(1024)S(1)}, f32[2048]{0:T(1024)}, u32[]{:S(2)}) copy-start(f32[2048]{0:T(1024)} %param.16) | copy-start | bytes 24580
  15.9 17.8 %collective-permute-start = (f32[1,8,128]{2,1,0:T(8,128)S(1)}, f32[1,8,128]{2,1,0:T(8,128)S(1)}, u32[]{:S(2)}, u32[]{:S(2)}) collective-permute-start(f32[1,8,128]{2,1,0:T(8,128)S(1)} %get-tuple-element.147), channel_id=1, source_target_pairs={{0,4},{4,8},{8,12},{12,16},{16,20},{20,24},{24,28},{28,32},{32,36}... | collective-permute-start | bytes 12296 | tf_op jit(solution)/shard_map/ppermute | solution.py:24
  18.7 15.1 %collective-permute-start.1 = (f32[1,8,128]{2,1,0:T(8,128)S(1)}, f32[1,8,128]{2,1,0:T(8,128)S(1)}, u32[]{:S(2)}, u32[]{:S(2)}) collective-permute-start(f32[1,8,128]{2,1,0:T(8,128)S(1)} %get-tuple-element.148), channel_id=1, source_target_pairs={{4,0},{8,4},{12,8},{16,12},{20,16},{24,20},{28,24},{32,28},{36,32}... | collective-permute-start | bytes 12296 | tf_op jit(solution)/shard_map/ppermute | solution.py:25
  19.4 14.3 %copy-start.18 = (s32[128]{0:T(128)}, s32[128]{0:T(128)S(1)}, u32[]{:S(2)}) copy-start(s32[128]{0:T(128)S(1)} %fusion.53) | copy-start | bytes 1540
  21.2 20.2 %all-to-all-start = ((s32[128,1,2]{2,1,0:T(1,128)}), s32[128,1,2]{2,1,0:T(1,128)S(1)}, u32[]{:S(2)}, u32[]{:S(2)}) async-start(s32[128,1,2]{2,1,0:T(1,128)} %bitcast.2), calls=%async_computation | async-start | bytes 131072 | tf_op jit(solution)/shard_map/all_to_all | solution.py:157
  31.8 11.8 %copy-start.16 = (pred[16]{0:T(512)(128)(4,1)}, pred[16]{0:T(512)(128)(4,1)S(1)}, u32[]{:S(2)}) copy-start(pred[16]{0:T(512)(128)(4,1)S(1)} %get-tuple-element.154) | copy-start | bytes 52
  33.8 9.6 %collective-permute-start.2 = (f32[18,1,128]{2,1,0:T(1,128)S(1)}, f32[18,1,128]{2,1,0:T(1,128)S(1)}, u32[]{:S(2)}, u32[]{:S(2)}) collective-permute-start(f32[18,1,128]{2,1,0:T(1,128)S(1)} %get-tuple-element.141), channel_id=1, source_target_pairs={{0,1},{1,2},{2,3},{3,0},{4,5},{5,6},{6,7},{7,4},{8,9},{9,10},{10,1... | collective-permute-start | bytes 27656 | tf_op jit(solution)/shard_map/ppermute | solution.py:24
  35.3 8.2 %collective-permute-start.3 = (f32[18,1,128]{2,1,0:T(1,128)S(1)}, f32[18,1,128]{2,1,0:T(1,128)S(1)}, u32[]{:S(2)}, u32[]{:S(2)}) collective-permute-start(f32[18,1,128]{2,1,0:T(1,128)S(1)} %get-tuple-element.142), channel_id=1, source_target_pairs={{1,0},{2,1},{3,2},{0,3},{5,4},{6,5},{7,6},{4,7},{9,8},{10,9},{11,1... | collective-permute-start | bytes 27656 | tf_op jit(solution)/shard_map/ppermute | solution.py:25
  50.4 6.6 %copy-start.6 = (f32[4,1,2,4,32,4]{5,4,3,2,1,0:T(8,128)S(1)}, f32[4,1,2,4,32,4]{5,4,3,2,1,0:T(8,128)}, u32[]{:S(2)}) copy-start(f32[4,1,2,4,32,4]{5,4,3,2,1,0:T(8,128)} %get-tuple-element.111) | copy-start | bytes 49156
  50.4 6.9 %copy-start.4 = (f32[4,1,2,4,32,4]{5,4,3,2,1,0:T(8,128)S(1)}, f32[4,1,2,4,32,4]{5,4,3,2,1,0:T(8,128)}, u32[]{:S(2)}) copy-start(f32[4,1,2,4,32,4]{5,4,3,2,1,0:T(8,128)} %get-tuple-element.114) | copy-start | bytes 49156
  50.4 7.2 %copy-start.2 = (f32[4,1,2,4,32,4]{5,4,3,2,1,0:T(8,128)S(1)}, f32[4,1,2,4,32,4]{5,4,3,2,1,0:T(8,128)}, u32[]{:S(2)}) copy-start(f32[4,1,2,4,32,4]{5,4,3,2,1,0:T(8,128)} %get-tuple-element.113) | copy-start | bytes 49156
  50.5 7.4 %copy-start.1 = (f32[4,1,2,4,32,4]{5,4,3,2,1,0:T(8,128)S(1)}, f32[4,1,2,4,32,4]{5,4,3,2,1,0:T(8,128)}, u32[]{:S(2)}) copy-start(f32[4,1,2,4,32,4]{5,4,3,2,1,0:T(8,128)} %get-tuple-element.112) | copy-start | bytes 49156
  59.5 3.7 %copy-start.10 = (s32[128,2]{1,0:T(8,128)S(1)}, s32[128,2]{1,0:T(8,128)}, u32[]{:S(2)}) copy-start(s32[128,2]{1,0:T(8,128)} %get-tuple-element.144) | copy-start | bytes 3076
  59.5 10.5 %copy-start.17 = (pred[16]{0:T(512)(128)(4,1)S(1)}, pred[16]{0:T(512)(128)(4,1)}, u32[]{:S(2)}) copy-start(pred[16]{0:T(512)(128)(4,1)} %copy-done.16) | copy-start | bytes 52
  60.4 9.8 %copy-start.19 = (s32[128]{0:T(128)S(1)}, s32[128]{0:T(128)}, u32[]{:S(2)}) copy-start(s32[128]{0:T(128)} %copy-done.18) | copy-start | bytes 1540
  60.4 34.0 %copy-start.8 = (bf16[4,2048]{1,0:T(4,128)(2,1)S(1)}, bf16[4,2048]{1,0:T(4,128)(2,1)}, u32[]{:S(2)}) copy-start(bf16[4,2048]{1,0:T(4,128)(2,1)} %param.13) | copy-start | bytes 49156
  60.4 34.0 %copy-start.11 = (bf16[512,4]{0,1:T(4,128)(2,1)S(1)}, bf16[512,4]{0,1:T(4,128)(2,1)}, u32[]{:S(2)}) copy-start(bf16[512,4]{0,1:T(4,128)(2,1)} %param.17) | copy-start | bytes 12292
  60.4 34.0 %copy-start.12 = (bf16[32,256,4]{1,2,0:T(4,128)(2,1)S(1)}, bf16[32,256,4]{1,2,0:T(4,128)(2,1)}, u32[]{:S(2)}) copy-start(bf16[32,256,4]{1,2,0:T(4,128)(2,1)} %custom-call.6) | copy-start | bytes 196612
  62.1 1.7 collective-permute-start.4
  63.1 3.0 %collective-permute-start.5 = (f32[1,8,128]{2,1,0:T(8,128)S(1)}, f32[1,8,128]{2,1,0:T(8,128)S(1)}, u32[]{:S(2)}, u32[]{:S(2)}) collective-permute-start(f32[1,8,128]{2,1,0:T(8,128)S(1)} %get-tuple-element.146), channel_id=1, source_target_pairs={{4,0},{8,4},{12,8},{16,12},{20,16},{24,20},{28,24},{32,28},{36,32}... | collective-permute-start | bytes 12296 | tf_op jit(solution)/shard_map/ppermute | solution.py:25
  66.2 3.8 %collective-permute-start.6 = (f32[18,1,128]{2,1,0:T(1,128)S(1)}, f32[18,1,128]{2,1,0:T(1,128)S(1)}, u32[]{:S(2)}, u32[]{:S(2)}) collective-permute-start(f32[18,1,128]{2,1,0:T(1,128)S(1)} %get-tuple-element.139), channel_id=1, source_target_pairs={{0,1},{1,2},{2,3},{3,0},{4,5},{5,6},{6,7},{7,4},{8,9},{9,10},{10,1... | collective-permute-start | bytes 27656 | tf_op jit(solution)/shard_map/ppermute | solution.py:24
  66.6 3.4 %collective-permute-start.7 = (f32[18,1,128]{2,1,0:T(1,128)S(1)}, f32[18,1,128]{2,1,0:T(1,128)S(1)}, u32[]{:S(2)}, u32[]{:S(2)}) collective-permute-start(f32[18,1,128]{2,1,0:T(1,128)S(1)} %get-tuple-element.140), channel_id=1, source_target_pairs={{1,0},{2,1},{3,2},{0,3},{5,4},{6,5},{7,6},{4,7},{9,8},{10,9},{11,1... | collective-permute-start | bytes 27656 | tf_op jit(solution)/shard_map/ppermute | solution.py:25
  71.7 21.1 %all-to-all-start.1 = ((bf16[128,2,128]{2,1,0:T(2,128)(2,1)}), bf16[128,2,128]{2,1,0:T(2,128)(2,1)S(1)}, u32[]{:S(2)}, u32[]{:S(2)}) async-start(bf16[128,2,128]{2,1,0:T(2,128)(2,1)} %bitcast.6), calls=%async_computation.1 | async-start | bytes 131072 | tf_op jit(solution)/shard_map/all_to_all | solution.py:150
  261.7 13.9 %all-to-all-start.2 = ((bf16[128,2,128]{2,1,0:T(2,128)(2,1)}), bf16[128,2,128]{2,1,0:T(2,128)(2,1)S(1)}, u32[]{:S(2)}, u32[]{:S(2)}) async-start(bf16[128,2,128]{2,1,0:T(2,128)(2,1)} %broadcast_select_fusion), calls=%async_computation.2 | async-start | bytes 131072 | tf_op jit(solution)/shard_map/all_to_all | solution.py:173
where the time goes:
time: 280 us; the launch traced here: 277 us
  matrix products  148 us (53%)
  local copies, waits for them, and re-layouts  38.3 us (14%)
  starting transfers between devices  35.7 us (13%)
  waiting for transfers between devices  27.9 us (10%)
  other arithmetic  25.3 us (9%)
    dot_general x32, matrix products, advance(): jnp.dot(hidden, w_hidden, preferred_element_type=jnp.float32)  73.9 us
    dot_general x32, matrix products, advance(): jnp.dot(level_in, w_state, preferred_element_type=jnp.float32)  67.6 us
    convert_element_type x32, other arithmetic, advance(): hidden = (jax.nn.sigmoid(output) * jnp.tanh(cell)).astype(jnp.bfloat16)  18 us
    unnamed x57, local copies, waits for them, and re-layouts  13.2 us
    all_to_all x1, starting transfers between devices, shards(): lax.all_to_all(outgoing.reshape(devices, capacity, channels), ('elem', 's...  11.4 us
    all_to_all x1, starting transfers between devices, shards(): lax.all_to_all(requests.reshape(devices, capacity), ('elem', 'span'), spl...  10.6 us
    all_to_all x1, waiting for transfers between devices, shards(): lax.all_to_all(outgoing.reshape(devices, capacity, channels), ('elem', 's...  9.67 us
    all_to_all x1, waiting for transfers between devices, shards(): lax.all_to_all(replies.reshape(devices, capacity, channels), ('elem', 'sp...  9.6 us
  transfers between devices with their start and end apart: 11, of which 6 were waited for; matrix products, arithmetic and copies ran while one was open for 2% of the time, Pallas kernels for 0%

commit v1 on v0

v1 whole, which is shorter than its diff:
```python
import math

import jax
import jax.numpy as jnp
import numpy as np
from jax import lax
from jax.experimental import pallas as pl
from jax.experimental.pallas import tpu as pltpu
from jax.sharding import PartitionSpec as P

NP = 4
NV = 4
HID = 512
LEVELS = 32
LANES = 128
COURANT = 0.05
F32 = jnp.float32
BF16 = jnp.bfloat16
VMEM_LIMIT = 48 << 20


def gll_table():
    nodes = np.array([-1.0, -1.0 / math.sqrt(5.0), 1.0 / math.sqrt(5.0), 1.0])
    width = nodes.shape[0]
    table = np.zeros((width, width))
    for row in range(width):
        for column in range(width):
            if row != column:
                upper = np.prod(
                    [nodes[row] - nodes[other] for other in range(width) if other != row]
                )
                lower = np.prod(
                    [nodes[column] - nodes[other] for other in range(width) if other != column]
                )
                table[row, column] = upper / (lower * (nodes[row] - nodes[column]))
            else:
                table[row, row] = sum(
                    (1.0 / (nodes[row] - nodes[other]) for other in range(width) if other != row)
                )
    return table


D = [[float(v) for v in row] for row in gll_table()]


def winds(f):
    flat = f.reshape(-1, LANES)
    v = lax.broadcasted_iota(jnp.int32, flat.shape, 1) % NV
    one = pltpu.roll(flat, 1, 1)
    two = pltpu.roll(flat, 2, 1)
    three = pltpu.roll(flat, 3, 1)
    back = pltpu.roll(flat, LANES - 1, 1)
    first = jnp.where(v == 0, flat, jnp.where(v == 1, one, jnp.where(v == 2, two, three)))
    second = jnp.where(v == 0, back, jnp.where(v == 1, flat, jnp.where(v == 2, one, two)))
    return first.reshape(f.shape), second.reshape(f.shape)


def along_x(f):
    rows = f.reshape(f.shape[0] // NP, NP, f.shape[1], LANES)
    pieces = []
    for i in range(NP):
        total = D[i][0] * rows[:, 0]
        for k in range(1, NP):
            total = total + D[i][k] * rows[:, k]
        pieces.append(total)
    return jnp.stack(pieces, axis=1).reshape(f.shape)


def along_y(f):
    size = f.shape[1]
    y = lax.broadcasted_iota(jnp.int32, (1, size, LANES), 1) % NP
    total = None
    for shift in range(-(NP - 1), NP):
        factor = jnp.zeros((1, size, LANES), F32)
        for i in range(NP):
            if 0 <= i + shift < NP:
                factor = jnp.where(y == i, D[i][i + shift], factor)
        moved = f if shift == 0 else pltpu.roll(f, (-shift) % size, 1)
        term = factor * moved
        total = term if total is None else total + term
    return total


def average_y(f, left, right):
    size = f.shape[1]
    y = lax.broadcasted_iota(jnp.int32, (1, size, LANES), 1)
    ahead = pltpu.roll(f, size - 1, 1)
    behind = pltpu.roll(f, 1, 1)
    other = jnp.where(y % NP == NP - 1, ahead, jnp.where(y % NP == 0, behind, f))
    other = jnp.where(y == size - 1, right, jnp.where(y == 0, left, other))
    return (f + other) * 0.5


def average_x(f, before, after):
    rows = f.shape[0]
    pieces = []
    for r in range(rows):
        if r % NP == 0:
            other = before if r == 0 else f[r - 1]
            pieces.append((f[r] + other) * 0.5)
        elif r % NP == NP - 1:
            other = after if r == rows - 1 else f[r + 1]
            pieces.append((f[r] + other) * 0.5)
        else:
            pieces.append(f[r])
    return jnp.stack(pieces, axis=0)


def first_kernel(state_ref, moved_ref, to_before_ref, to_after_ref):
    f = state_ref[...]
    wind_x, wind_y = winds(f)
    a = f - COURANT * (wind_x * along_x(f) + wind_y * along_y(f))
    moved_ref[...] = a
    n = a.shape[0]
    to_before_ref[0] = a[0]
    to_before_ref[1] = D[0][1] * a[1] + D[0][2] * a[2] + D[0][3] * ((a[3] + a[4]) * 0.5)
    to_after_ref[0] = a[n - 1]
    to_after_ref[1] = (
        D[3][0] * ((a[n - 4] + a[n - 5]) * 0.5) + D[3][1] * a[n - 3] + D[3][2] * a[n - 2]
    )


def second_kernel(moved_ref, before_ref, after_ref, g_ref, to_left_ref, to_right_ref):
    g = average_x(moved_ref[...], before_ref[0], after_ref[0])
    g_ref[...] = g
    rows, size, _ = g.shape
    middle = (g[:, 3] + g[:, 4]) * 0.5
    to_left_ref[0:rows] = g[:, 0]
    to_left_ref[rows : 2 * rows] = D[0][1] * g[:, 1] + D[0][2] * g[:, 2] + D[0][3] * middle
    to_right_ref[0:rows] = g[:, size - 1]
    to_right_ref[rows : 2 * rows] = (
        D[3][0] * middle + D[3][1] * g[:, size - 3] + D[3][2] * g[:, size - 2]
    )
    up, down = before_ref[1], after_ref[1]
    y = lax.broadcasted_iota(jnp.int32, (size, LANES), 0)
    to_left_ref[2 * rows : 2 * rows + 8] = jnp.where(
        y == 0, up, jnp.where(y == 1, pltpu.roll(down, 1, 0), 0.0)
    )
    to_right_ref[2 * rows : 2 * rows + 8] = jnp.where(
        y == 0, pltpu.roll(up, 1, 0), jnp.where(y == 1, pltpu.roll(down, 2, 0), 0.0)
    )


def third_kernel(g_ref, before_ref, after_ref, left_ref, right_ref, field_ref):
    g = g_ref[...]
    rows, size, _ = g.shape
    left_g = left_ref[0:rows].reshape(rows, 1, LANES)
    right_g = right_ref[0:rows].reshape(rows, 1, LANES)
    f = average_y(g, left_g, right_g)
    tail_l = left_ref[2 * rows : 2 * rows + 8]
    tail_r = right_ref[2 * rows : 2 * rows + 8]
    up = average_y(before_ref[1:2], tail_l[0:1].reshape(1, 1, LANES), tail_r[0:1].reshape(1, 1, LANES))[0]
    down = average_y(after_ref[1:2], tail_l[1:2].reshape(1, 1, LANES), tail_r[1:2].reshape(1, 1, LANES))[0]
    slope_x = average_x(
        along_x(f), D[3][3] * f[0] + up, D[0][0] * f[rows - 1] + down
    )
    other_l = left_ref[rows : 2 * rows].reshape(rows, 1, LANES)
    other_r = right_ref[rows : 2 * rows].reshape(rows, 1, LANES)
    slope_y = average_y(along_y(f), D[3][3] * f + other_l, D[0][0] * f + other_r)
    wind_x, wind_y = winds(f)
    field_ref[...] = f - COURANT * (wind_x * slope_x + wind_y * slope_y)


def weights_kernel(state_w_ref, surf_w_ref, hidden_w_ref, bias_ref, out_w_ref, w_ref, o_ref):
    lane = lax.broadcasted_iota(jnp.int32, (1, 4 * HID), 1)
    scale = jnp.where((lane >= 2 * HID) & (lane < 3 * HID), 1.0, 0.5)
    w_ref[0:HID] = (hidden_w_ref[...].astype(F32) * scale).astype(BF16)
    row = lax.broadcasted_iota(jnp.int32, (64, NV), 0)
    col = lax.broadcasted_iota(jnp.int32, (64, NV), 1)
    spread = (row % NV == col).astype(BF16)
    tiled = jnp.dot(spread, state_w_ref[...], preferred_element_type=F32)
    w_ref[HID : HID + 64] = (tiled * scale).astype(BF16)
    rest = bias_ref[...] * scale
    high = rest.astype(BF16).astype(F32)
    rest = rest - high
    mid = rest.astype(BF16).astype(F32)
    low = rest - mid
    r = lax.broadcasted_iota(jnp.int32, (16, 1), 0)
    parts = jnp.where(r == 0, high, jnp.where(r == 1, mid, jnp.where(r == 2, low, 0.0)))
    w_ref[HID + 64 : HID + 80] = parts.astype(BF16)
    w_ref[HID + 80 : HID + 96] = (surf_w_ref[...].astype(F32) * scale).astype(BF16)
    w_ref[HID + 96 : HID + 128] = jnp.zeros((32, 4 * HID), BF16)
    row = lax.broadcasted_iota(jnp.int32, (NV, LANES), 0)
    col = lax.broadcasted_iota(jnp.int32, (NV, LANES), 1)
    spread = (col % NV == row).astype(BF16)
    o_ref[...] = jnp.dot(out_w_ref[...], spread, preferred_element_type=F32).astype(BF16)


def lstm_kernel(slots_ref, table_ref, field_ref, w_ref, o_ref, out_ref, cell_ref, gain_ref):
    rows = field_ref.shape[0]
    feature_lane = lax.broadcasted_iota(jnp.int32, (16, LANES), 1)

    def fetch(c, acc):
        slot = slots_ref[c]
        owner = lax.shift_right_logical(slot, 8)
        place = jnp.bitwise_and(slot, 255)
        half = pl.multiple_of(jnp.bitwise_and(place, 128), 128)
        tile = table_ref[owner, :, pl.ds(half, LANES)].astype(F32)
        shift = jnp.bitwise_and(c - place + 256, 127)
        return jnp.where(feature_lane == c, pltpu.roll(tile, shift, 1), acc)

    surf = lax.fori_loop(0, rows, fetch, jnp.zeros((16, LANES), F32), unroll=8)
    surf = jnp.concatenate(
        [jnp.zeros((80, LANES), F32), surf, jnp.zeros((32, LANES), F32)], axis=0
    ).T
    lane = lax.broadcasted_iota(jnp.int32, (rows, LANES), 1)
    fixed = jnp.where((lane >= 64) & (lane < 67), 1.0, surf)
    field = field_ref[...]
    swapped = pltpu.roll(field, 64, 1)
    unit = 256

    def level_input(level):
        source = jnp.where(level < LEVELS // 2, field, swapped)
        return jnp.where(lane // NV == level % (LEVELS // 2), source, fixed).astype(BF16)

    def gates(x, h, j):
        out = []
        for q in range(4):
            s = slice(q * HID + j * unit, q * HID + (j + 1) * unit)
            g = jnp.dot(x, w_ref[HID : HID + LANES, s], preferred_element_type=F32)
            if h is not None:
                g = g + jnp.dot(h, w_ref[0:HID, s], preferred_element_type=F32)
            out.append(g)
        return out

    def cell_step(g, j, first):
        s = slice(j * unit, (j + 1) * unit)
        c = (0.5 * jnp.tanh(g[0]) + 0.5) * jnp.tanh(g[2])
        if not first:
            c = c + (0.5 * jnp.tanh(g[1]) + 0.5) * cell_ref[:, s]
        cell_ref[:, s] = c
        return ((0.5 * jnp.tanh(g[3]) + 0.5) * jnp.tanh(c)).astype(BF16)

    def emit(h, level):
        p = jnp.dot(h, o_ref[...], preferred_element_type=F32)
        gain_ref[...] = jnp.where(lane // NV == level, p, gain_ref[...])

    def step(level, h, first=False):
        x = level_input(level)
        new = [cell_step(gates(x, h, j), j, first) for j in range(HID // unit)]
        new = jnp.concatenate(new, axis=1)
        emit(new, level)
        return new

    gain_ref[...] = jnp.zeros_like(gain_ref)
    h = step(0, None, True)
    lax.fori_loop(1, LEVELS, step, h)
    out_ref[...] = field + gain_ref[...].astype(BF16).astype(F32)


def call(kernel, out_shape, *args, smem=(), scratch=(), cost=None):
    return pl.pallas_call(
        kernel,
        out_shape=out_shape,
        in_specs=[
            pl.BlockSpec(memory_space=pltpu.SMEM if i in smem else pltpu.VMEM)
            for i in range(len(args))
        ],
        out_specs=jax.tree.map(lambda _: pl.BlockSpec(memory_space=pltpu.VMEM), out_shape),
        scratch_shapes=list(scratch),
        compiler_params=pltpu.CompilerParams(vmem_limit_bytes=VMEM_LIMIT),
        cost_estimate=cost,
    )(*args)


def like(*shape, dtype=F32):
    return jax.ShapeDtypeStruct(shape, dtype)


def exchange(to_lower, to_upper, axis):
    size = lax.axis_size(axis)
    up = [(i, (i + 1) % size) for i in range(size)]
    down = [(j, i) for i, j in up]
    return lax.ppermute(to_upper, axis, up), lax.ppermute(to_lower, axis, down)


def shards(state, assignment, surface, w_state, w_surf, w_hidden, bias, w_out):
    node_rows, node_cols, channels = state.shape
    devices = lax.axis_size("elem") * lax.axis_size("span")
    columns_here = node_rows * node_cols
    slot_count, features = surface.shape
    table = lax.all_to_all(
        jnp.broadcast_to(surface.T[None], (devices, features, slot_count)),
        ("elem", "span"),
        split_axis=0,
        concat_axis=0,
        tiled=True,
    )
    block = like(node_rows, node_cols, channels)
    edge = like(2, node_cols, channels)
    moved, to_before, to_after = call(first_kernel, (block, edge, edge), state)
    before, after = exchange(to_before, to_after, "elem")
    side = like(2 * node_rows + 8, channels)
    g, to_left, to_right = call(second_kernel, (block, side, side), moved, before, after)
    left, right = exchange(to_left, to_right, "span")
    field = call(third_kernel, block, g, before, after, left, right)
    weights, out_weights = call(
        weights_kernel,
        (like(HID + LANES, 4 * HID, dtype=BF16), like(HID, LANES, dtype=BF16)),
        w_state,
        w_surf,
        w_hidden,
        bias.reshape(1, 4 * HID),
        w_out,
    )
    result = call(
        lstm_kernel,
        like(columns_here, channels),
        assignment.reshape(columns_here),
        table,
        field.reshape(columns_here, channels),
        weights,
        out_weights,
        smem=(0,),
        scratch=(pltpu.VMEM((columns_here, HID), F32), pltpu.VMEM((columns_here, channels), F32)),
    )
    return result.reshape(node_rows, node_cols, channels)


def solution(mesh):
    placed = (
        P("elem", "span", None),
        P("elem", "span"),
        P(("elem", "span"), None),
        P(),
        P(),
        P(),
        P(),
        P(),
    )
    return jax.shard_map(
        shards, mesh=mesh, in_specs=placed, out_specs=P("elem", "span", None), check_vma=False
    )
```

time: 280 us -> 66.2 us (0.24)
  the two profiles are of different devices: /device:TPU:1 before, /device:TPU:0 now
where the time goes in v1:
time: 66.2 us; the launch traced here: 65.8 us
  Pallas kernels  28.5 us (43%)
  starting transfers between devices  25.9 us (39%)
  local copies, waits for them, and re-layouts  8.03 us (12%)
  waiting for transfers between devices  3.24 us (5%)
    pallas_call x5, Pallas kernels, call(): pl.pallas_call(kernel, out_shape=out_shape, in_specs=[pl.BlockSpec(memory...  28.5 us
    all_to_all x1, starting transfers between devices, shards(): lax.all_to_all(jnp.broadcast_to(surface.T[None], (devices, features, slot...  11.2 us
    ppermute x2, starting transfers between devices, exchange(): lax.ppermute(to_lower, axis, down)  8.21 us
    ppermute x2, starting transfers between devices, exchange(): lax.ppermute(to_upper, axis, up)  6.55 us
    unnamed x22, local copies, waits for them, and re-layouts  5.53 us
    ppermute x2, waiting for transfers between devices, exchange(): lax.ppermute(to_upper, axis, up)  3.23 us
    broadcast_in_dim x1, local copies, waits for them, and re-layouts, shards(): jnp.broadcast_to(surface.T[None], (devices, features, slot_count))  1.88 us
  transfers between devices with their start and end apart: 5, of which 1 were waited for; matrix products, arithmetic and copies ran while one was open for 1% of the time, Pallas kernels for 4%

profile of v1, /device:TPU:0, one launch (start us, length us, event | category | flops | bytes accessed | tf_op | source)
XLA Modules:
  0.0 65.8 jit_solution(6532158902081017795)
XLA Ops:
  0.0 1.9 %broadcast_in_dim.2 = bf16[128,16,256]{2,1,0:T(8,128)(2,1)} broadcast(bf16[16,256]{1,0:T(8,128)(2,1)} %bitcast.6), dimensions={1,2} | broadcast | bytes 1056768 | tf_op jit(solution)/shard_map/broadcast_in_dim | solution.py:283
  1.9 11.2 %all-to-all-start = ((bf16[128,16,256]{2,1,0:T(8,128)(2,1)}), bf16[128,16,256]{2,1,0:T(8,128)(2,1)S(1)}, u32[]{:S(2)}, u32[]{:S(2)}) async-start(bf16[128,16,256]{2,1,0:T(8,128)(2,1)} %broadcast_in_dim.2), calls=%async_computation | async-start | bytes 2097152 | tf_op jit(solution)/shard_map/all_to_all | solution.py:282
  13.1 0.0 copy-done.4
  13.1 0.1 shard_map.82
  13.2 0.1 collective-permute-start
  13.3 5.1 %collective-permute-start.1 = (f32[2,8,128]{2,1,0:T(8,128)S(1)}, f32[2,8,128]{2,1,0:T(8,128)S(1)}, u32[]{:S(2)}, u32[]{:S(2)}) collective-permute-start(f32[2,8,128]{2,1,0:T(8,128)S(1)} %get-tuple-element.15), channel_id=1, source_target_pairs={{4,0},{8,4},{12,8},{16,12},{20,16},{24,20},{28,24},{32,28},{36,32}... | collective-permute-start | bytes 24584 | tf_op jit(solution)/shard_map/ppermute | solution.py:274
  18.3 3.2 %collective-permute-done.before_ref = f32[2,8,128]{2,1,0:T(8,128)S(1)} collective-permute-done((f32[2,8,128]{2,1,0:T(8,128)S(1)}, f32[2,8,128]{2,1,0:T(8,128)S(1)}, u32[]{:S(2)}, u32[]{:S(2)}) %collective-permute-start) | collective-permute-done | bytes 8224 | tf_op jit(solution)/shard_map/ppermute | solution.py:274
  21.6 0.0 collective-permute-done.1.after_ref
  21.6 0.7 %shard_map.83 = (f32[16,8,128]{2,1,0:T(8,128)S(1)}, f32[40,128]{1,0:T(8,128)}, f32[40,128]{1,0:T(8,128)}) custom-call(f32[16,8,128]{2,1,0:T(8,128)S(1)} %get-tuple-element.13.moved_ref, f32[2,8,128]{2,1,0:T(8,128)S(1)} %collective-permute-done.before_ref, f32[2,8,128]{2,1,0:T(8,128)S(1)} %collective-permute-done.1.after_ref), custom_call_target="tpu_custom_call" | custom-call | tf_op jit(solution)/shard_map/pallas_call | solution.py:252
  22.2 6.5 %collective-permute-start.2 = (f32[40,128]{1,0:T(8,128)}, f32[40,128]{1,0:T(8,128)}, u32[]{:S(2)}, u32[]{:S(2)}) collective-permute-start(f32[40,128]{1,0:T(8,128)} %get-tuple-element.17), channel_id=1, source_target_pairs={{0,1},{1,2},{2,3},{3,0},{4,5},{5,6},{6,7},{7,4},{8,9},{9,10},{10,1... | collective-permute-start | bytes 61448 | tf_op jit(solution)/shard_map/ppermute | solution.py:274
  28.7 3.2 %collective-permute-start.3 = (f32[40,128]{1,0:T(8,128)}, f32[40,128]{1,0:T(8,128)}, u32[]{:S(2)}, u32[]{:S(2)}) collective-permute-start(f32[40,128]{1,0:T(8,128)} %get-tuple-element.18), channel_id=1, source_target_pairs={{1,0},{2,1},{3,2},{0,3},{5,4},{6,5},{7,6},{4,7},{9,8},{10,9},{11,1... | collective-permute-start | bytes 61448 | tf_op jit(solution)/shard_map/ppermute | solution.py:274
  31.9 0.0 copy-done.8
  31.9 0.1 copy.11
  32.0 0.6 reshape.13.slots_ref
  32.6 0.0 copy-done.9
  32.6 0.2 copy.12.out_w_ref
  32.8 0.0 copy-done.2
  32.8 0.0 copy-done.3
  32.8 0.0 copy-start.5
  32.8 0.7 %copy-done.5 = bf16[4,2048]{1,0:T(4,128)(2,1)S(1)} copy-done((bf16[4,2048]{1,0:T(4,128)(2,1)S(1)}, bf16[4,2048]{1,0:T(4,128)(2,1)}, u32[]{:S(2)}) %copy-start.5) | copy-done | bytes 16408
  33.5 0.7 %copy-done.6 = f32[2048]{0:T(1024)S(1)} copy-done((f32[2048]{0:T(1024)S(1)}, f32[2048]{0:T(1024)}, u32[]{:S(2)}) %copy-start.6) | copy-done | bytes 8216
  34.2 0.9 %shard_map.85 = (bf16[640,2048]{1,0:T(8,128)(2,1)S(1)}, bf16[512,128]{1,0:T(8,128)(2,1)S(1)}) custom-call(bf16[4,2048]{1,0:T(4,128)(2,1)S(1)} %copy-done.5, bf16[16,2048]{1,0:T(8,128)(2,1)S(1)} %copy-done.3, bf16[512,2048]{1,0:T(8,128)(2,1)S(1)} %copy-done.2, f32[1,2048]{1,0:T(1,128)S(1)} %bitcast.5, bf16[512,4]{1,0:T(8,128)(2,1)S(1)} %copy.12.out_w_ref), custom_call_target="tpu_custom_call" | custom-call | tf_op jit(solution)/shard_map/pallas_call | solution.py:252
  35.1 0.0 copy-start
  35.1 1.5 %copy-done = bf16[640,2048]{1,0:T(8,128)(2,1)} copy-done((bf16[640,2048]{1,0:T(8,128)(2,1)}, bf16[640,2048]{1,0:T(8,128)(2,1)S(1)}, u32[]{:S(2)}) %copy-start) | copy-done | bytes 2621464
  36.6 0.0 collective-permute-done.2.left_ref
  36.6 0.0 collective-permute-done.3.right_ref
  36.6 0.9 %shard_map.84 = f32[16,8,128]{2,1,0:T(8,128)S(1)} custom-call(f32[16,8,128]{2,1,0:T(8,128)S(1)} %get-tuple-element.16.g_ref, f32[2,8,128]{2,1,0:T(8,128)S(1)} %collective-permute-done.before_ref, f32[2,8,128]{2,1,0:T(8,128)S(1)} %collective-permute-done.1.after_ref, f32[40,128]{1,0:T(8,128)} %collective-permute-done.2.left_ref, ...), custom_call_target="tpu_custom_call" | custom-call | tf_op jit(solution)/shard_map/pallas_call | solution.py:252
  37.5 0.0 all-to-all-done.table_ref
  37.5 0.0 copy-start.1
  37.5 1.7 %copy-done.1 = bf16[640,2048]{1,0:T(8,128)(2,1)S(1)} copy-done((bf16[640,2048]{1,0:T(8,128)(2,1)S(1)}, bf16[640,2048]{1,0:T(8,128)(2,1)}, u32[]{:S(2)}) %copy-start.1) | copy-done | bytes 2621464
  39.3 0.6 copy-done.7
  39.9 25.9 %shard_map.86 = f32[128,128]{1,0:T(8,128)} custom-call(s32[128]{0:T(128)S(1)} %copy-done.7, bf16[128,16,256]{2,1,0:T(8,128)(2,1)S(1)} %all-to-all-done.table_ref, f32[128,128]{1,0:T(8,128)S(1)} %bitcast.4, bf16[640,2048]{1,0:T(8,128)(2,1)S(1)} %copy-done.1, bf16[512,128]{1,0:T(8,128)(2,1)S(1)} %get-tuple-element.20.o_ref), custom_call_target="tpu_custom_call" | custom-call | tf_op jit(solution)/shard_map/pallas_call | solution.py:252
  (7 shorter events, 0.0 us)
Async XLA Ops:
  0.0 13.1 %copy-start.4 = (f32[16,8,128]{2,1,0:T(8,128)S(1)}, f32[16,8,128]{2,1,0:T(8,128)}, u32[]{:S(2)}) copy-start(f32[16,8,128]{2,1,0:T(8,128)} %state_ref.1) | copy-start | bytes 196612
  0.0 31.9 %copy-start.8 = (s32[16,8]{0,1:T(8,128)S(1)}, s32[16,8]{0,1:T(8,128)}, u32[]{:S(2)}) copy-start(s32[16,8]{0,1:T(8,128)} %param.9) | copy-start | bytes 1540
  0.0 32.6 %copy-start.9 = (bf16[512,4]{0,1:T(4,128)(2,1)S(1)}, bf16[512,4]{0,1:T(4,128)(2,1)}, u32[]{:S(2)}) copy-start(bf16[512,4]{0,1:T(4,128)(2,1)} %param.15) | copy-start | bytes 12292
  0.0 32.8 %copy-start.2 = (bf16[512,2048]{1,0:T(8,128)(2,1)S(1)}, bf16[512,2048]{1,0:T(8,128)(2,1)}, u32[]{:S(2)}) copy-start(bf16[512,2048]{1,0:T(8,128)(2,1)} %hidden_w_ref.1) | copy-start | bytes 6291460
  0.0 32.8 %copy-start.3 = (bf16[16,2048]{1,0:T(8,128)(2,1)S(1)}, bf16[16,2048]{1,0:T(8,128)(2,1)}, u32[]{:S(2)}) copy-start(bf16[16,2048]{1,0:T(8,128)(2,1)} %surf_w_ref.1) | copy-start | bytes 196612
  1.9 35.6 %all-to-all-start = ((bf16[128,16,256]{2,1,0:T(8,128)(2,1)}), bf16[128,16,256]{2,1,0:T(8,128)(2,1)S(1)}, u32[]{:S(2)}, u32[]{:S(2)}) async-start(bf16[128,16,256]{2,1,0:T(8,128)(2,1)} %broadcast_in_dim.2), calls=%async_computation | async-start | bytes 2097152 | tf_op jit(solution)/shard_map/all_to_all | solution.py:282
  13.2 8.4 %collective-permute-start = (f32[2,8,128]{2,1,0:T(8,128)S(1)}, f32[2,8,128]{2,1,0:T(8,128)S(1)}, u32[]{:S(2)}, u32[]{:S(2)}) collective-permute-start(f32[2,8,128]{2,1,0:T(8,128)S(1)} %get-tuple-element.14), channel_id=1, source_target_pairs={{0,4},{4,8},{8,12},{12,16},{16,20},{20,24},{24,28},{28,32},{32,36}... | collective-permute-start | bytes 24584 | tf_op jit(solution)/shard_map/ppermute | solution.py:274
  13.3 8.3 %collective-permute-start.1 = (f32[2,8,128]{2,1,0:T(8,128)S(1)}, f32[2,8,128]{2,1,0:T(8,128)S(1)}, u32[]{:S(2)}, u32[]{:S(2)}) collective-permute-start(f32[2,8,128]{2,1,0:T(8,128)S(1)} %get-tuple-element.15), channel_id=1, source_target_pairs={{4,0},{8,4},{12,8},{16,12},{20,16},{24,20},{28,24},{32,28},{36,32}... | collective-permute-start | bytes 24584 | tf_op jit(solution)/shard_map/ppermute | solution.py:274
  22.2 14.3 %collective-permute-start.2 = (f32[40,128]{1,0:T(8,128)}, f32[40,128]{1,0:T(8,128)}, u32[]{:S(2)}, u32[]{:S(2)}) collective-permute-start(f32[40,128]{1,0:T(8,128)} %get-tuple-element.17), channel_id=1, source_target_pairs={{0,1},{1,2},{2,3},{3,0},{4,5},{5,6},{6,7},{7,4},{8,9},{9,10},{10,1... | collective-permute-start | bytes 61448 | tf_op jit(solution)/shard_map/ppermute | solution.py:274
  28.7 7.8 %collective-permute-start.3 = (f32[40,128]{1,0:T(8,128)}, f32[40,128]{1,0:T(8,128)}, u32[]{:S(2)}, u32[]{:S(2)}) collective-permute-start(f32[40,128]{1,0:T(8,128)} %get-tuple-element.18), channel_id=1, source_target_pairs={{1,0},{2,1},{3,2},{0,3},{5,4},{6,5},{7,6},{4,7},{9,8},{10,9},{11,1... | collective-permute-start | bytes 61448 | tf_op jit(solution)/shard_map/ppermute | solution.py:274
  32.8 0.7 %copy-start.5 = (bf16[4,2048]{1,0:T(4,128)(2,1)S(1)}, bf16[4,2048]{1,0:T(4,128)(2,1)}, u32[]{:S(2)}) copy-start(bf16[4,2048]{1,0:T(4,128)(2,1)} %state_w_ref.1) | copy-start | bytes 49156
  33.5 0.7 %copy-start.6 = (f32[2048]{0:T(1024)S(1)}, f32[2048]{0:T(1024)}, u32[]{:S(2)}) copy-start(f32[2048]{0:T(1024)} %param.14) | copy-start | bytes 24580
  35.1 1.5 %copy-start = (bf16[640,2048]{1,0:T(8,128)(2,1)}, bf16[640,2048]{1,0:T(8,128)(2,1)S(1)}, u32[]{:S(2)}) copy-start(bf16[640,2048]{1,0:T(8,128)(2,1)S(1)} %get-tuple-element.19.w_ref) | copy-start | bytes 7864324
  37.5 1.7 %copy-start.1 = (bf16[640,2048]{1,0:T(8,128)(2,1)S(1)}, bf16[640,2048]{1,0:T(8,128)(2,1)}, u32[]{:S(2)}) copy-start(bf16[640,2048]{1,0:T(8,128)(2,1)} %copy-done) | copy-start | bytes 7864324
  39.3 0.6 copy-start.7

commit v2 on v1

--- a/solution.py
+++ b/solution.py
@@ -16,7 +16,7 @@
 COURANT = 0.05
 F32 = jnp.float32
 BF16 = jnp.bfloat16
-VMEM_LIMIT = 48 << 20
+VMEM_LIMIT = 16 << 20
 
 
 def gll_table():
@@ -106,7 +106,8 @@
     return jnp.stack(pieces, axis=0)
 
 
-def first_kernel(state_ref, moved_ref, to_before_ref, to_after_ref):
+def first_kernel(state_ref, surface_ref, moved_ref, to_before_ref, to_after_ref, spread_ref):
+    spread_ref[...] = jnp.broadcast_to(surface_ref[...][None], spread_ref.shape)
     f = state_ref[...]
     wind_x, wind_y = winds(f)
     a = f - COURANT * (wind_x * along_x(f) + wind_y * along_y(f))
@@ -161,41 +162,43 @@
     field_ref[...] = f - COURANT * (wind_x * slope_x + wind_y * slope_y)
 
 
-def weights_kernel(state_w_ref, surf_w_ref, hidden_w_ref, bias_ref, out_w_ref, w_ref, o_ref):
-    lane = lax.broadcasted_iota(jnp.int32, (1, 4 * HID), 1)
-    scale = jnp.where((lane >= 2 * HID) & (lane < 3 * HID), 1.0, 0.5)
-    w_ref[0:HID] = (hidden_w_ref[...].astype(F32) * scale).astype(BF16)
+def lstm_kernel(
+    slots_ref, core_ref, near_ref, far_ref, field_ref, state_w_ref, surf_w_ref, hidden_w_ref, bias_ref, out_w_ref,
+    out_ref, in_w_ref, cell_ref, part_ref, pend_ref, past_ref,
+):
+    rows = field_ref.shape[0]
+    gates = 4 * HID
+    unit = HID // 2
     row = lax.broadcasted_iota(jnp.int32, (64, NV), 0)
     col = lax.broadcasted_iota(jnp.int32, (64, NV), 1)
     spread = (row % NV == col).astype(BF16)
-    tiled = jnp.dot(spread, state_w_ref[...], preferred_element_type=F32)
-    w_ref[HID : HID + 64] = (tiled * scale).astype(BF16)
-    rest = bias_ref[...] * scale
-    high = rest.astype(BF16).astype(F32)
-    rest = rest - high
+    in_w_ref[0:64] = jnp.dot(spread, state_w_ref[...], preferred_element_type=F32).astype(BF16)
+    bias = bias_ref[...]
+    high = bias.astype(BF16).astype(F32)
+    rest = bias - high
     mid = rest.astype(BF16).astype(F32)
     low = rest - mid
     r = lax.broadcasted_iota(jnp.int32, (16, 1), 0)
     parts = jnp.where(r == 0, high, jnp.where(r == 1, mid, jnp.where(r == 2, low, 0.0)))
-    w_ref[HID + 64 : HID + 80] = parts.astype(BF16)
-    w_ref[HID + 80 : HID + 96] = (surf_w_ref[...].astype(F32) * scale).astype(BF16)
-    w_ref[HID + 96 : HID + 128] = jnp.zeros((32, 4 * HID), BF16)
-    row = lax.broadcasted_iota(jnp.int32, (NV, LANES), 0)
-    col = lax.broadcasted_iota(jnp.int32, (NV, LANES), 1)
-    spread = (col % NV == row).astype(BF16)
-    o_ref[...] = jnp.dot(out_w_ref[...], spread, preferred_element_type=F32).astype(BF16)
-
-
-def lstm_kernel(slots_ref, table_ref, field_ref, w_ref, o_ref, out_ref, cell_ref, gain_ref):
-    rows = field_ref.shape[0]
+    in_w_ref[64:80] = parts.astype(BF16)
+    in_w_ref[80:96] = surf_w_ref[...]
+    in_w_ref[96:128] = jnp.zeros((32, gates), BF16)
+
     feature_lane = lax.broadcasted_iota(jnp.int32, (16, LANES), 1)
+    core = core_ref[0]
 
     def fetch(c, acc):
-        slot = slots_ref[c]
+        slot = slots_ref[jnp.bitwise_and(c, 7), lax.shift_right_logical(c, 3)]
         owner = lax.shift_right_logical(slot, 8)
         place = jnp.bitwise_and(slot, 255)
         half = pl.multiple_of(jnp.bitwise_and(place, 128), 128)
-        tile = table_ref[owner, :, pl.ds(half, LANES)].astype(F32)
+        index = jnp.bitwise_or(
+            lax.shift_left(lax.shift_right_logical(owner, 3), 2), jnp.bitwise_and(owner, 3)
+        )
+        here = jnp.bitwise_and(lax.shift_right_logical(owner, 2), 1) == core
+        near = near_ref[index, :, pl.ds(half, LANES)]
+        far = far_ref[index, :, pl.ds(half, LANES)]
+        tile = jnp.where(here, near, far).astype(F32)
         shift = jnp.bitwise_and(c - place + 256, 127)
         return jnp.where(feature_lane == c, pltpu.roll(tile, shift, 1), acc)
 
@@ -204,48 +207,72 @@
         [jnp.zeros((80, LANES), F32), surf, jnp.zeros((32, LANES), F32)], axis=0
     ).T
     lane = lax.broadcasted_iota(jnp.int32, (rows, LANES), 1)
-    fixed = jnp.where((lane >= 64) & (lane < 67), 1.0, surf)
+    fixed = jnp.where((lane >= 64) & (lane < 67), 0.5, 0.5 * surf)
     field = field_ref[...]
-    swapped = pltpu.roll(field, 64, 1)
-    unit = 256
+    half_field = 0.5 * field.astype(BF16).astype(F32)
+    swapped = pltpu.roll(half_field, 64, 1)
 
     def level_input(level):
-        source = jnp.where(level < LEVELS // 2, field, swapped)
+        source = jnp.where(level < LEVELS // 2, half_field, swapped)
         return jnp.where(lane // NV == level % (LEVELS // 2), source, fixed).astype(BF16)
 
-    def gates(x, h, j):
-        out = []
-        for q in range(4):
-            s = slice(q * HID + j * unit, q * HID + (j + 1) * unit)
-            g = jnp.dot(x, w_ref[HID : HID + LANES, s], preferred_element_type=F32)
-            if h is not None:
-                g = g + jnp.dot(h, w_ref[0:HID, s], preferred_element_type=F32)
-            out.append(g)
-        return out
-
-    def cell_step(g, j, first):
+    def dot(a, b):
+        return jnp.dot(a, b, preferred_element_type=F32)
+
+    def cols(q, j):
+        return slice(q * HID + j * unit, q * HID + (j + 1) * unit)
+
+    def cell_step(g, j, first=False):
         s = slice(j * unit, (j + 1) * unit)
-        c = (0.5 * jnp.tanh(g[0]) + 0.5) * jnp.tanh(g[2])
+        c = (0.5 * jnp.tanh(g[0]) + 0.5) * jnp.tanh(g[2] + g[2])
         if not first:
             c = c + (0.5 * jnp.tanh(g[1]) + 0.5) * cell_ref[:, s]
         cell_ref[:, s] = c
-        return ((0.5 * jnp.tanh(g[3]) + 0.5) * jnp.tanh(c)).astype(BF16)
-
-    def emit(h, level):
-        p = jnp.dot(h, o_ref[...], preferred_element_type=F32)
-        gain_ref[...] = jnp.where(lane // NV == level, p, gain_ref[...])
-
-    def step(level, h, first=False):
+        return ((0.25 * jnp.tanh(g[3]) + 0.25) * jnp.tanh(c)).astype(BF16)
+
+    x = level_input(0)
+    low_half = cell_step([dot(x, in_w_ref[:, cols(q, 0)]) for q in range(4)], 0, True)
+    for q in range(4):
+        pend_ref[q] = dot(x, in_w_ref[:, cols(q, 1)])
+    cell_ref[:, unit:HID] = jnp.zeros((rows, unit), F32)
+
+    def finish(level, low_half):
+        high_half = cell_step([pend_ref[q] for q in range(4)], 1)
+        past_ref[level] = jnp.concatenate([low_half, high_half], axis=1)
+        return high_half
+
+    def step(level, low_half):
         x = level_input(level)
-        new = [cell_step(gates(x, h, j), j, first) for j in range(HID // unit)]
-        new = jnp.concatenate(new, axis=1)
-        emit(new, level)
+        for j in range(2):
+            for q in range(4):
+                part_ref[j, q] = dot(x, in_w_ref[:, cols(q, j)]) + dot(
+                    low_half, hidden_w_ref[0:unit, cols(q, j)]
+                )
+        high_half = finish(level - 1, low_half)
+        g = [
+            part_ref[0, q] + dot(high_half, hidden_w_ref[unit:HID, cols(q, 0)]) for q in range(4)
+        ]
+        new = cell_step(g, 0)
+        for q in range(4):
+            pend_ref[q] = part_ref[1, q] + dot(high_half, hidden_w_ref[unit:HID, cols(q, 1)])
         return new
 
-    gain_ref[...] = jnp.zeros_like(gain_ref)
-    h = step(0, None, True)
-    lax.fori_loop(1, LEVELS, step, h)
-    out_ref[...] = field + gain_ref[...].astype(BF16).astype(F32)
+    low_half = lax.fori_loop(1, LEVELS, step, low_half, unroll=4)
+    finish(LEVELS - 1, low_half)
+    row = lax.broadcasted_iota(jnp.int32, (NV, LANES), 0)
+    col = lax.broadcasted_iota(jnp.int32, (NV, LANES), 1)
+    spread = (col % NV == row).astype(BF16)
+    out_w = lax.dot_general(
+        out_w_ref[...], spread, (((0,), (0,)), ((), ())), preferred_element_type=F32
+    )
+    out_w = (out_w + out_w).astype(BF16)
+    group = 8
+    gain = jnp.zeros((rows, LANES), F32)
+    for k in range(LEVELS // group):
+        p = dot(past_ref[k * group : (k + 1) * group].reshape(group * rows, HID), out_w)
+        for i in range(group):
+            gain = jnp.where(lane // NV == k * group + i, p[i * rows : (i + 1) * rows], gain)
+    out_ref[...] = field + gain.astype(BF16).astype(F32)
 
 
 def call(kernel, out_shape, *args, smem=(), scratch=(), cost=None):
@@ -267,61 +294,70 @@
     return jax.ShapeDtypeStruct(shape, dtype)
 
 
-def exchange(to_lower, to_upper, axis):
-    size = lax.axis_size(axis)
+ALL = ("z", "y", "c", "x")
+ELEM = ("z", "y", "c")
+
+
+def exchange(to_lower, to_upper, axes):
+    size = math.prod(lax.axis_size(a) for a in axes)
     up = [(i, (i + 1) % size) for i in range(size)]
     down = [(j, i) for i, j in up]
-    return lax.ppermute(to_upper, axis, up), lax.ppermute(to_lower, axis, down)
+    return lax.ppermute(to_upper, axes, up), lax.ppermute(to_lower, axes, down)
 
 
 def shards(state, assignment, surface, w_state, w_surf, w_hidden, bias, w_out):
     node_rows, node_cols, channels = state.shape
-    devices = lax.axis_size("elem") * lax.axis_size("span")
     columns_here = node_rows * node_cols
     slot_count, features = surface.shape
-    table = lax.all_to_all(
-        jnp.broadcast_to(surface.T[None], (devices, features, slot_count)),
-        ("elem", "span"),
-        split_axis=0,
-        concat_axis=0,
-        tiled=True,
-    )
+    peers = lax.axis_size("z") * lax.axis_size("y") * lax.axis_size("x")
     block = like(node_rows, node_cols, channels)
     edge = like(2, node_cols, channels)
-    moved, to_before, to_after = call(first_kernel, (block, edge, edge), state)
-    before, after = exchange(to_before, to_after, "elem")
+    moved, to_before, to_after, spread = call(
+        first_kernel,
+        (block, edge, edge, like(peers, features, slot_count, dtype=BF16)),
+        state,
+        surface.T,
+    )
+    before, after = exchange(to_before, to_after, ELEM)
+    near = lax.all_to_all(spread, ("z", "y", "x"), split_axis=0, concat_axis=0, tiled=True)
+    far = lax.ppermute(near, "c", [(0, 1), (1, 0)])
     side = like(2 * node_rows + 8, channels)
     g, to_left, to_right = call(second_kernel, (block, side, side), moved, before, after)
-    left, right = exchange(to_left, to_right, "span")
+    left, right = exchange(to_left, to_right, ("x",))
     field = call(third_kernel, block, g, before, after, left, right)
-    weights, out_weights = call(
-        weights_kernel,
-        (like(HID + LANES, 4 * HID, dtype=BF16), like(HID, LANES, dtype=BF16)),
+    core = lax.axis_index("c").reshape(1)
+    result = call(
+        lstm_kernel,
+        like(columns_here, channels),
+        assignment.T,
+        core,
+        near,
+        far,
+        field.reshape(columns_here, channels),
         w_state,
         w_surf,
         w_hidden,
         bias.reshape(1, 4 * HID),
-        w_out,
-    )
-    result = call(
-        lstm_kernel,
-        like(columns_here, channels),
-        assignment.reshape(columns_here),
-        table,
-        field.reshape(columns_here, channels),
-        weights,
-        out_weights,
-        smem=(0,),
-        scratch=(pltpu.VMEM((columns_here, HID), F32), pltpu.VMEM((columns_here, channels), F32)),
+        w_out.T,
+        smem=(0, 1),
+        scratch=(
+            pltpu.VMEM((LANES, 4 * HID), BF16),
+            pltpu.VMEM((columns_here, HID), F32),
+            pltpu.VMEM((2, 4, columns_here, HID // 2), F32),
+            pltpu.VMEM((4, columns_here, HID // 2), F32),
+            pltpu.VMEM((LEVELS, columns_here, HID), BF16),
+        ),
     )
     return result.reshape(node_rows, node_cols, channels)
 
 
 def solution(mesh):
+    devices = mesh.devices
+    mesh = jax.sharding.Mesh(devices.reshape(4, 4, 2, 4), ALL)
     placed = (
-        P("elem", "span", None),
-        P("elem", "span"),
-        P(("elem", "span"), None),
+        P(ELEM, "x", None),
+        P(ELEM, "x"),
+        P(ALL, None),
         P(),
         P(),
         P(),
@@ -329,5 +365,5 @@
         P(),
     )
     return jax.shard_map(
-        shards, mesh=mesh, in_specs=placed, out_specs=P("elem", "span", None), check_vma=False
-    )
+        shards, mesh=mesh, in_specs=placed, out_specs=P(ELEM, "x", None), check_vma=False
+    )

time: 66.2 us -> 66 us (level)
  the two profiles are of different devices: /device:TPU:0 before, /device:TPU:6 now
where the time goes in v2:
time: 66 us; the launch traced here: 65.6 us
  blocking collectives  22.7 us (34%)
  Pallas kernels  22.2 us (34%)
  starting transfers between devices  7.48 us (11%)
  local copies, waits for them, and re-layouts  6.75 us (10%)
  waiting for transfers between devices  6.36 us (10%)
    all_to_all x1, blocking collectives, shards(): lax.all_to_all(spread, ('z', 'y', 'x'), split_axis=0, concat_axis=0, tile...  22.7 us
    pallas_call x4, Pallas kernels, call(): pl.pallas_call(kernel, out_shape=out_shape, in_specs=[pl.BlockSpec(memory...  22.2 us
    unnamed x16, local copies, waits for them, and re-layouts  6.75 us
    ppermute x2, starting transfers between devices, exchange(): lax.ppermute(to_lower, axes, down)  4.56 us
    ppermute x2, waiting for transfers between devices, exchange(): lax.ppermute(to_lower, axes, down)  3.55 us
    ppermute x2, starting transfers between devices, exchange(): lax.ppermute(to_upper, axes, up)  2.92 us
    ppermute x2, waiting for transfers between devices, exchange(): lax.ppermute(to_upper, axes, up)  2.81 us
  transfers between devices with their start and end apart: 5, of which 3 were waited for; matrix products, arithmetic and copies ran while one was open for 0% of the time, Pallas kernels for 0%

profile of v2, /device:TPU:6, one launch (start us, length us, event | category | flops | bytes accessed | tf_op | source)
XLA Modules:
  0.0 65.6 jit_solution(3432206135750401444)
XLA Ops:
  0.0 0.0 copy-start.2
  0.0 0.8 %copy-done.2 = f32[16,8,128]{2,1,0:T(8,128)S(1)} copy-done((f32[16,8,128]{2,1,0:T(8,128)S(1)}, f32[16,8,128]{2,1,0:T(8,128)}, u32[]{:S(2)}) %copy-start.2) | copy-done | bytes 65560
  0.8 0.0 copy-start.5
  0.8 0.7 %copy-done.5 = bf16[256,16]{0,1:T(8,128)(2,1)S(1)} copy-done((bf16[256,16]{0,1:T(8,128)(2,1)S(1)}, bf16[256,16]{0,1:T(8,128)(2,1)}, u32[]{:S(2)}) %copy-start.5) | copy-done | bytes 8216
  1.5 0.2 shard_map.82
  1.7 22.7 %all_to_all.5.near_ref = bf16[64,16,256]{2,1,0:T(8,128)(2,1)S(1)} all-to-all(bf16[64,16,256]{2,1,0:T(8,128)(2,1)S(1)} %get-tuple-element.12), channel_id=1, replica_groups=mesh['z'=4,'y'=4,'c'=2,'x'=4] {'z','y','x'}, dimensions={0} | all-to-all | bytes 1048576 | tf_op jit(solution)/shard_map/all_to_all | solution.py:322
  24.4 0.0 collective-permute-start
  24.4 0.5 collective-permute-start.1
  24.9 4.6 %collective-permute-start.2 = (f32[2,8,128]{2,1,0:T(8,128)S(1)}, f32[2,8,128]{2,1,0:T(8,128)S(1)}, u32[]{:S(2)}, u32[]{:S(2)}) collective-permute-start(f32[2,8,128]{2,1,0:T(8,128)S(1)} %get-tuple-element.15), channel_id=1, source_target_pairs={{4,0},{8,4},{12,8},{16,12},{20,16},{24,20},{28,24},{32,28},{36,32}... | collective-permute-start | bytes 24584 | tf_op jit(solution)/shard_map/ppermute | solution.py:305
  29.5 1.3 %collective-permute-done.1.before_ref = f32[2,8,128]{2,1,0:T(8,128)S(1)} collective-permute-done((f32[2,8,128]{2,1,0:T(8,128)S(1)}, f32[2,8,128]{2,1,0:T(8,128)S(1)}, u32[]{:S(2)}, u32[]{:S(2)}) %collective-permute-start.1) | collective-permute-done | bytes 8224 | tf_op jit(solution)/shard_map/ppermute | solution.py:305
  30.8 0.0 collective-permute-done.2.after_ref
  30.9 0.1 shard_map.83
  30.9 2.4 %collective-permute-start.3 = (f32[40,128]{1,0:T(8,128)S(1)}, f32[40,128]{1,0:T(8,128)S(1)}, u32[]{:S(2)}, u32[]{:S(2)}) collective-permute-start(f32[40,128]{1,0:T(8,128)S(1)} %get-tuple-element.17), channel_id=1, source_target_pairs={{0,1},{1,2},{2,3},{3,0},{4,5},{5,6},{6,7},{7,4},{8,9},{9,10},{10,1... | collective-permute-start | bytes 61448 | tf_op jit(solution)/shard_map/ppermute | solution.py:305
  33.3 0.0 collective-permute-start.4
  33.3 1.5 %collective-permute-done.3.left_ref = f32[40,128]{1,0:T(8,128)S(1)} collective-permute-done((f32[40,128]{1,0:T(8,128)S(1)}, f32[40,128]{1,0:T(8,128)S(1)}, u32[]{:S(2)}, u32[]{:S(2)}) %collective-permute-start.3) | collective-permute-done | bytes 20512 | tf_op jit(solution)/shard_map/ppermute | solution.py:305
  34.8 3.5 %collective-permute-done.4.right_ref = f32[40,128]{1,0:T(8,128)S(1)} collective-permute-done((f32[40,128]{1,0:T(8,128)S(1)}, f32[40,128]{1,0:T(8,128)S(1)}, u32[]{:S(2)}, u32[]{:S(2)}) %collective-permute-start.4) | collective-permute-done | bytes 20512 | tf_op jit(solution)/shard_map/ppermute | solution.py:305
  38.3 0.2 shard_map.84
  38.5 0.0 collective-permute-done.far_ref
  38.5 0.0 copy-start
  38.5 1.6 %copy-done = bf16[512,2048]{1,0:T(8,128)(2,1)S(1)} copy-done((bf16[512,2048]{1,0:T(8,128)(2,1)S(1)}, bf16[512,2048]{1,0:T(8,128)(2,1)}, u32[]{:S(2)}) %copy-start) | copy-done | bytes 2097176
  40.1 0.0 copy-start.1
  40.1 0.8 %copy-done.1 = bf16[16,2048]{1,0:T(8,128)(2,1)S(1)} copy-done((bf16[16,2048]{1,0:T(8,128)(2,1)S(1)}, bf16[16,2048]{1,0:T(8,128)(2,1)}, u32[]{:S(2)}) %copy-start.1) | copy-done | bytes 65560
  41.0 0.0 copy-start.3
  41.0 0.7 %copy-done.3 = bf16[4,2048]{1,0:T(4,128)(2,1)S(1)} copy-done((bf16[4,2048]{1,0:T(4,128)(2,1)S(1)}, bf16[4,2048]{1,0:T(4,128)(2,1)}, u32[]{:S(2)}) %copy-start.3) | copy-done | bytes 16408
  41.7 0.0 copy-start.4
  41.7 0.7 %copy-done.4 = f32[2048]{0:T(1024)S(1)} copy-done((f32[2048]{0:T(1024)S(1)}, f32[2048]{0:T(1024)}, u32[]{:S(2)}) %copy-start.4) | copy-done | bytes 8216
  42.4 0.0 copy-start.6
  42.4 0.7 %copy-done.6 = s32[16,8]{0,1:T(8,128)S(1)} copy-done((s32[16,8]{0,1:T(8,128)S(1)}, s32[16,8]{0,1:T(8,128)}, u32[]{:S(2)}) %copy-start.6) | copy-done | bytes 536
  43.1 0.0 copy-start.7
  43.1 0.7 %copy-done.7 = bf16[512,4]{0,1:T(4,128)(2,1)S(1)} copy-done((bf16[512,4]{0,1:T(4,128)(2,1)S(1)}, bf16[512,4]{0,1:T(4,128)(2,1)}, u32[]{:S(2)}) %copy-start.7) | copy-done | bytes 4120
  43.8 21.8 %shard_map.85 = f32[128,128]{1,0:T(8,128)} custom-call(s32[8,16]{1,0:T(8,128)S(1)} %bitcast.10, s32[1]{0:T(128)} %bitcast.1.core_ref, bf16[64,16,256]{2,1,0:T(8,128)(2,1)S(1)} %all_to_all.5.near_ref, bf16[64,16,256]{2,1,0:T(8,128)(2,1)S(1)} %collective-permute-done.far_ref, f32[128,128]{1,0:T(8,128)S(1)} %bitcast.7, bf16[4,2048]{1,0:T(4,128)(2,1)S(1)} %copy-done.3, ...), custom_call_target="tpu_custom_call" | custom-call | tf_op jit(solution)/shard_map/pallas_call | solution.py:279
Async XLA Ops:
  0.0 0.8 %copy-start.2 = (f32[16,8,128]{2,1,0:T(8,128)S(1)}, f32[16,8,128]{2,1,0:T(8,128)}, u32[]{:S(2)}) copy-start(f32[16,8,128]{2,1,0:T(8,128)} %state_ref.1) | copy-start | bytes 196612
  0.8 0.7 %copy-start.5 = (bf16[256,16]{0,1:T(8,128)(2,1)S(1)}, bf16[256,16]{0,1:T(8,128)(2,1)}, u32[]{:S(2)}) copy-start(bf16[256,16]{0,1:T(8,128)(2,1)} %param.10) | copy-start | bytes 24580
  24.4 14.1 %collective-permute-start = (bf16[64,16,256]{2,1,0:T(8,128)(2,1)S(1)}, bf16[64,16,256]{2,1,0:T(8,128)(2,1)S(1)}, u32[]{:S(2)}, u32[]{:S(2)}) collective-permute-start(bf16[64,16,256]{2,1,0:T(8,128)(2,1)S(1)} %all_to_all.5.near_ref), channel_id=1, source_target_pairs={{0,4},{4,0},{1,5},{5,1},{2,6},{6,2},{3,7},{7,3},{8,12},{12,8},{9,1... | collective-permute-start | bytes 1572872 | tf_op jit(solution)/shard_map/ppermute | solution.py:323
  24.4 6.4 %collective-permute-start.1 = (f32[2,8,128]{2,1,0:T(8,128)S(1)}, f32[2,8,128]{2,1,0:T(8,128)S(1)}, u32[]{:S(2)}, u32[]{:S(2)}) collective-permute-start(f32[2,8,128]{2,1,0:T(8,128)S(1)} %get-tuple-element.14), channel_id=1, source_target_pairs={{0,4},{4,8},{8,12},{12,16},{16,20},{20,24},{24,28},{28,32},{32,36}... | collective-permute-start | bytes 24584 | tf_op jit(solution)/shard_map/ppermute | solution.py:305
  24.9 5.9 %collective-permute-start.2 = (f32[2,8,128]{2,1,0:T(8,128)S(1)}, f32[2,8,128]{2,1,0:T(8,128)S(1)}, u32[]{:S(2)}, u32[]{:S(2)}) collective-permute-start(f32[2,8,128]{2,1,0:T(8,128)S(1)} %get-tuple-element.15), channel_id=1, source_target_pairs={{4,0},{8,4},{12,8},{16,12},{20,16},{24,20},{28,24},{32,28},{36,32}... | collective-permute-start | bytes 24584 | tf_op jit(solution)/shard_map/ppermute | solution.py:305
  30.9 3.9 %collective-permute-start.3 = (f32[40,128]{1,0:T(8,128)S(1)}, f32[40,128]{1,0:T(8,128)S(1)}, u32[]{:S(2)}, u32[]{:S(2)}) collective-permute-start(f32[40,128]{1,0:T(8,128)S(1)} %get-tuple-element.17), channel_id=1, source_target_pairs={{0,1},{1,2},{2,3},{3,0},{4,5},{5,6},{6,7},{7,4},{8,9},{9,10},{10,1... | collective-permute-start | bytes 61448 | tf_op jit(solution)/shard_map/ppermute | solution.py:305
  33.3 5.0 %collective-permute-start.4 = (f32[40,128]{1,0:T(8,128)S(1)}, f32[40,128]{1,0:T(8,128)S(1)}, u32[]{:S(2)}, u32[]{:S(2)}) collective-permute-start(f32[40,128]{1,0:T(8,128)S(1)} %get-tuple-element.18), channel_id=1, source_target_pairs={{1,0},{2,1},{3,2},{0,3},{5,4},{6,5},{7,6},{4,7},{9,8},{10,9},{11,1... | collective-permute-start | bytes 61448 | tf_op jit(solution)/shard_map/ppermute | solution.py:305
  38.5 1.6 %copy-start = (bf16[512,2048]{1,0:T(8,128)(2,1)S(1)}, bf16[512,2048]{1,0:T(8,128)(2,1)}, u32[]{:S(2)}) copy-start(bf16[512,2048]{1,0:T(8,128)(2,1)} %hidden_w_ref.1) | copy-start | bytes 6291460
  40.1 0.8 %copy-start.1 = (bf16[16,2048]{1,0:T(8,128)(2,1)S(1)}, bf16[16,2048]{1,0:T(8,128)(2,1)}, u32[]{:S(2)}) copy-start(bf16[16,2048]{1,0:T(8,128)(2,1)} %surf_w_ref.1) | copy-start | bytes 196612
  41.0 0.7 %copy-start.3 = (bf16[4,2048]{1,0:T(4,128)(2,1)S(1)}, bf16[4,2048]{1,0:T(4,128)(2,1)}, u32[]{:S(2)}) copy-start(bf16[4,2048]{1,0:T(4,128)(2,1)} %state_w_ref.1) | copy-start | bytes 49156
  41.7 0.7 %copy-start.4 = (f32[2048]{0:T(1024)S(1)}, f32[2048]{0:T(1024)}, u32[]{:S(2)}) copy-start(f32[2048]{0:T(1024)} %param.14) | copy-start | bytes 24580
  42.4 0.7 %copy-start.6 = (s32[16,8]{0,1:T(8,128)S(1)}, s32[16,8]{0,1:T(8,128)}, u32[]{:S(2)}) copy-start(s32[16,8]{0,1:T(8,128)} %param.9) | copy-start | bytes 1540
  43.1 0.7 %copy-start.7 = (bf16[512,4]{0,1:T(4,128)(2,1)S(1)}, bf16[512,4]{0,1:T(4,128)(2,1)}, u32[]{:S(2)}) copy-start(bf16[512,4]{0,1:T(4,128)(2,1)} %param.15) | copy-start | bytes 12292

commit v3 on v2

--- a/solution.py
+++ b/solution.py
@@ -106,9 +106,18 @@
     return jnp.stack(pieces, axis=0)
 
 
-def first_kernel(state_ref, surface_ref, moved_ref, to_before_ref, to_after_ref, spread_ref):
-    spread_ref[...] = jnp.broadcast_to(surface_ref[...][None], spread_ref.shape)
-    f = state_ref[...]
+def spread_kernel(surface_ref, spread_ref, here_ref, arrived):
+    copy = pltpu.make_async_copy(surface_ref, here_ref, arrived)
+    copy.start()
+    copy.wait()
+    spread_ref[...] = jnp.broadcast_to(here_ref[...][None], spread_ref.shape)
+
+
+def first_kernel(state_ref, moved_ref, to_before_ref, to_after_ref, here_ref, arrived):
+    copy = pltpu.make_async_copy(state_ref, here_ref, arrived)
+    copy.start()
+    copy.wait()
+    f = here_ref[...]
     wind_x, wind_y = winds(f)
     a = f - COURANT * (wind_x * along_x(f) + wind_y * along_y(f))
     moved_ref[...] = a
@@ -163,12 +172,22 @@
 
 
 def lstm_kernel(
-    slots_ref, core_ref, near_ref, far_ref, field_ref, state_w_ref, surf_w_ref, hidden_w_ref, bias_ref, out_w_ref,
-    out_ref, in_w_ref, cell_ref, part_ref, pend_ref, past_ref,
+    near_ref, far_ref, field_ref, *refs
 ):
+    kept, out_ref = refs[:6], refs[6]
+    slots_ref, state_w_ref, surf_w_ref, hidden_w_ref, bias_ref, out_w_ref = refs[7:13]
+    in_w_ref, cell_ref, part_ref, pend_ref, past_ref, arrived = refs[13:]
+    copies = [
+        pltpu.make_async_copy(source, target, arrived.at[i])
+        for i, (source, target) in enumerate(zip(kept, refs[7:13]))
+    ]
+    for copy in copies:
+        copy.start()
     rows = field_ref.shape[0]
     gates = 4 * HID
     unit = HID // 2
+    for i in (1, 2, 4):
+        copies[i].wait()
     row = lax.broadcasted_iota(jnp.int32, (64, NV), 0)
     col = lax.broadcasted_iota(jnp.int32, (64, NV), 1)
     spread = (row % NV == col).astype(BF16)
@@ -185,7 +204,8 @@
     in_w_ref[96:128] = jnp.zeros((32, gates), BF16)
 
     feature_lane = lax.broadcasted_iota(jnp.int32, (16, LANES), 1)
-    core = core_ref[0]
+    core = jnp.bitwise_and(lax.axis_index("c"), 1)
+    copies[0].wait()
 
     def fetch(c, acc):
         slot = slots_ref[jnp.bitwise_and(c, 7), lax.shift_right_logical(c, 3)]
@@ -257,8 +277,10 @@
             pend_ref[q] = part_ref[1, q] + dot(high_half, hidden_w_ref[unit:HID, cols(q, 1)])
         return new
 
+    copies[3].wait()
     low_half = lax.fori_loop(1, LEVELS, step, low_half, unroll=4)
     finish(LEVELS - 1, low_half)
+    copies[5].wait()
     row = lax.broadcasted_iota(jnp.int32, (NV, LANES), 0)
     col = lax.broadcasted_iota(jnp.int32, (NV, LANES), 1)
     spread = (col % NV == row).astype(BF16)
@@ -275,12 +297,14 @@
     out_ref[...] = field + gain.astype(BF16).astype(F32)
 
 
-def call(kernel, out_shape, *args, smem=(), scratch=(), cost=None):
+def call(kernel, out_shape, *args, kept=(), scratch=(), cost=None):
+    placed = len(args)
+    args = (*args, *[pltpu.with_memory_space_constraint(a, pltpu.HBM) for a in kept])
     return pl.pallas_call(
         kernel,
         out_shape=out_shape,
         in_specs=[
-            pl.BlockSpec(memory_space=pltpu.SMEM if i in smem else pltpu.VMEM)
+            pl.BlockSpec(memory_space=pltpu.VMEM if i < placed else pltpu.HBM)
             for i in range(len(args))
         ],
         out_specs=jax.tree.map(lambda _: pl.BlockSpec(memory_space=pltpu.VMEM), out_shape),
@@ -312,40 +336,43 @@
     peers = lax.axis_size("z") * lax.axis_size("y") * lax.axis_size("x")
     block = like(node_rows, node_cols, channels)
     edge = like(2, node_cols, channels)
-    moved, to_before, to_after, spread = call(
+    spread = call(
+        spread_kernel,
+        like(peers, features, slot_count, dtype=BF16),
+        kept=(surface.T,),
+        scratch=(pltpu.VMEM((features, slot_count), BF16), pltpu.SemaphoreType.DMA(())),
+    )
+    moved, to_before, to_after = call(
         first_kernel,
-        (block, edge, edge, like(peers, features, slot_count, dtype=BF16)),
-        state,
-        surface.T,
+        (block, edge, edge),
+        kept=(state,),
+        scratch=(pltpu.VMEM(state.shape, F32), pltpu.SemaphoreType.DMA(())),
     )
     before, after = exchange(to_before, to_after, ELEM)
     near = lax.all_to_all(spread, ("z", "y", "x"), split_axis=0, concat_axis=0, tiled=True)
-    far = lax.ppermute(near, "c", [(0, 1), (1, 0)])
     side = like(2 * node_rows + 8, channels)
     g, to_left, to_right = call(second_kernel, (block, side, side), moved, before, after)
     left, right = exchange(to_left, to_right, ("x",))
     field = call(third_kernel, block, g, before, after, left, right)
-    core = lax.axis_index("c").reshape(1)
+    near, _ = lax.optimization_barrier((near, field))
+    far = lax.ppermute(near, "c", [(0, 1), (1, 0)])
+    kept = (assignment.T, w_state, w_surf, w_hidden, bias.reshape(1, 4 * HID), w_out.T)
     result = call(
         lstm_kernel,
         like(columns_here, channels),
-        assignment.T,
-        core,
         near,
         far,
         field.reshape(columns_here, channels),
-        w_state,
-        w_surf,
-        w_hidden,
-        bias.reshape(1, 4 * HID),
-        w_out.T,
-        smem=(0, 1),
+        kept=kept,
         scratch=(
+            pltpu.SMEM(kept[0].shape, kept[0].dtype),
+            *[pltpu.VMEM(a.shape, a.dtype) for a in kept[1:]],
             pltpu.VMEM((LANES, 4 * HID), BF16),
             pltpu.VMEM((columns_here, HID), F32),
             pltpu.VMEM((2, 4, columns_here, HID // 2), F32),
             pltpu.VMEM((4, columns_here, HID // 2), F32),
             pltpu.VMEM((LEVELS, columns_here, HID), BF16),
+            pltpu.SemaphoreType.DMA((len(kept),)),
         ),
     )
     return result.reshape(node_rows, node_cols, channels)

time: 66 us -> 52.9 us (0.80)
  the two profiles are of different devices: /device:TPU:6 before, /device:TPU:1 now
where the time goes in v3:
time: 52.9 us; the launch traced here: 52.6 us
  Pallas kernels  24.9 us (47%)
  starting transfers between devices  21 us (40%)
  waiting for transfers between devices  6.71 us (13%)
    pallas_call x5, Pallas kernels, call(): pl.pallas_call(kernel, out_shape=out_shape, in_specs=[pl.BlockSpec(memory...  24.9 us
    all_to_all x1, starting transfers between devices, shards(): lax.all_to_all(spread, ('z', 'y', 'x'), split_axis=0, concat_axis=0, tile...  12 us
    ppermute x2, starting transfers between devices, exchange(): lax.ppermute(to_upper, axes, up)  4.02 us
    ppermute x1, starting transfers between devices, shards(): far = lax.ppermute(near, 'c', [(0, 1), (1, 0)])  3.35 us
    ppermute x2, waiting for transfers between devices, exchange(): lax.ppermute(to_lower, axes, down)  2.65 us
    ppermute x2, waiting for transfers between devices, exchange(): lax.ppermute(to_upper, axes, up)  2.17 us
    ppermute x2, starting transfers between devices, exchange(): lax.ppermute(to_lower, axes, down)  1.63 us
    ppermute x1, waiting for transfers between devices, shards(): far = lax.ppermute(near, 'c', [(0, 1), (1, 0)])  1.54 us
  transfers between devices with their start and end apart: 6, of which 5 were waited for; matrix products, arithmetic and copies ran while one was open for 0% of the time, Pallas kernels for 2%

profile of v3, /device:TPU:1, one launch (start us, length us, event | category | flops | bytes accessed | tf_op | source)
XLA Modules:
  0.0 52.6 jit_solution(11972918228649321561)
XLA Ops:
  0.0 1.5 %shard_map.82 = bf16[64,16,256]{2,1,0:T(8,128)(2,1)} custom-call(bf16[16,256]{1,0:T(8,128)(2,1)} %bitcast.7), custom_call_target="tpu_custom_call" | custom-call | tf_op jit(solution)/shard_map/pallas_call | solution.py:303
  1.5 12.0 %all-to-all-start = ((bf16[64,16,256]{2,1,0:T(8,128)(2,1)}), bf16[64,16,256]{2,1,0:T(8,128)(2,1)S(1)}, u32[]{:S(2)}, u32[]{:S(2)}) async-start(bf16[64,16,256]{2,1,0:T(8,128)(2,1)} %shard_map.82), calls=%async_computation | async-start | bytes 1048576 | tf_op jit(solution)/shard_map/all_to_all | solution.py:352
  13.5 1.0 %shard_map.83 = (f32[16,8,128]{2,1,0:T(8,128)S(1)}, f32[2,8,128]{2,1,0:T(8,128)S(1)}, f32[2,8,128]{2,1,0:T(8,128)S(1)}) custom-call(f32[16,8,128]{2,1,0:T(8,128)} %state_ref.1), custom_call_target="tpu_custom_call" | custom-call | tf_op jit(solution)/shard_map/pallas_call | solution.py:303
  14.5 2.2 %collective-permute-start = (f32[2,8,128]{2,1,0:T(8,128)S(1)}, f32[2,8,128]{2,1,0:T(8,128)S(1)}, u32[]{:S(2)}, u32[]{:S(2)}) collective-permute-start(f32[2,8,128]{2,1,0:T(8,128)S(1)} %get-tuple-element.13), channel_id=1, source_target_pairs={{0,4},{4,8},{8,12},{12,16},{16,20},{20,24},{24,28},{28,32},{32,36}... | collective-permute-start | bytes 24584 | tf_op jit(solution)/shard_map/ppermute | solution.py:329
  16.7 0.0 collective-permute-start.1
  16.7 0.8 %collective-permute-done.before_ref = f32[2,8,128]{2,1,0:T(8,128)S(1)} collective-permute-done((f32[2,8,128]{2,1,0:T(8,128)S(1)}, f32[2,8,128]{2,1,0:T(8,128)S(1)}, u32[]{:S(2)}, u32[]{:S(2)}) %collective-permute-start) | collective-permute-done | bytes 8224 | tf_op jit(solution)/shard_map/ppermute | solution.py:329
  17.5 2.6 %collective-permute-done.1.after_ref = f32[2,8,128]{2,1,0:T(8,128)S(1)} collective-permute-done((f32[2,8,128]{2,1,0:T(8,128)S(1)}, f32[2,8,128]{2,1,0:T(8,128)S(1)}, u32[]{:S(2)}, u32[]{:S(2)}) %collective-permute-start.1) | collective-permute-done | bytes 8224 | tf_op jit(solution)/shard_map/ppermute | solution.py:329
  20.2 0.1 shard_map.84
  20.2 1.8 %collective-permute-start.2 = (f32[40,128]{1,0:T(8,128)S(1)}, f32[40,128]{1,0:T(8,128)S(1)}, u32[]{:S(2)}, u32[]{:S(2)}) collective-permute-start(f32[40,128]{1,0:T(8,128)S(1)} %get-tuple-element.16), channel_id=1, source_target_pairs={{0,1},{1,2},{2,3},{3,0},{4,5},{5,6},{6,7},{7,4},{8,9},{9,10},{10,1... | collective-permute-start | bytes 61448 | tf_op jit(solution)/shard_map/ppermute | solution.py:329
  22.1 1.6 %collective-permute-start.3 = (f32[40,128]{1,0:T(8,128)S(1)}, f32[40,128]{1,0:T(8,128)S(1)}, u32[]{:S(2)}, u32[]{:S(2)}) collective-permute-start(f32[40,128]{1,0:T(8,128)S(1)} %get-tuple-element.17), channel_id=1, source_target_pairs={{1,0},{2,1},{3,2},{0,3},{5,4},{6,5},{7,6},{4,7},{9,8},{10,9},{11,1... | collective-permute-start | bytes 61448 | tf_op jit(solution)/shard_map/ppermute | solution.py:329
  23.7 1.4 %collective-permute-done.2.left_ref = f32[40,128]{1,0:T(8,128)S(1)} collective-permute-done((f32[40,128]{1,0:T(8,128)S(1)}, f32[40,128]{1,0:T(8,128)S(1)}, u32[]{:S(2)}, u32[]{:S(2)}) %collective-permute-start.2) | collective-permute-done | bytes 20512 | tf_op jit(solution)/shard_map/ppermute | solution.py:329
  25.1 0.0 collective-permute-done.3.right_ref
  25.1 0.2 shard_map.85
  25.3 0.3 all-to-all-done.near_ref
  25.6 3.3 %collective-permute-start.4 = (bf16[64,16,256]{2,1,0:T(8,128)(2,1)S(1)}, bf16[64,16,256]{2,1,0:T(8,128)(2,1)S(1)}, u32[]{:S(2)}, u32[]{:S(2)}) collective-permute-start(bf16[64,16,256]{2,1,0:T(8,128)(2,1)S(1)} %all-to-all-done.near_ref), channel_id=1, source_target_pairs={{0,4},{4,0},{1,5},{5,1},{2,6},{6,2},{3,7},{7,3},{8,12},{12,8},{9,1... | collective-permute-start | bytes 1572872 | tf_op jit(solution)/shard_map/ppermute | solution.py:358
  29.0 1.5 %collective-permute-done.4.far_ref = bf16[64,16,256]{2,1,0:T(8,128)(2,1)S(1)} collective-permute-done((bf16[64,16,256]{2,1,0:T(8,128)(2,1)S(1)}, bf16[64,16,256]{2,1,0:T(8,128)(2,1)S(1)}, u32[]{:S(2)}, u32[]{:S(2)}) %collective-permute-start.4) | collective-permute-done | bytes 524320 | tf_op jit(solution)/shard_map/ppermute | solution.py:358
  30.5 22.1 %shard_map.86 = f32[128,128]{1,0:T(8,128)} custom-call(bf16[64,16,256]{2,1,0:T(8,128)(2,1)S(1)} %all-to-all-done.near_ref, bf16[64,16,256]{2,1,0:T(8,128)(2,1)S(1)} %collective-permute-done.4.far_ref, f32[128,128]{1,0:T(8,128)S(1)} %bitcast.6, s32[8,16]{1,0:T(8,128)} %bitcast.9, bf16[4,2048]{1,0:T(4,128)(2,1)} %refs_1_.1, bf16[16,2048]{1,0:T(8,128)(2,1)} %refs_2_.1, ...), custom_call_target="tpu_custom_call" | custom-call | tf_op jit(solution)/shard_map/pallas_call | solution.py:303
Async XLA Ops:
  1.5 24.1 %all-to-all-start = ((bf16[64,16,256]{2,1,0:T(8,128)(2,1)}), bf16[64,16,256]{2,1,0:T(8,128)(2,1)S(1)}, u32[]{:S(2)}, u32[]{:S(2)}) async-start(bf16[64,16,256]{2,1,0:T(8,128)(2,1)} %shard_map.82), calls=%async_computation | async-start | bytes 1048576 | tf_op jit(solution)/shard_map/all_to_all | solution.py:352
  14.5 3.0 %collective-permute-start = (f32[2,8,128]{2,1,0:T(8,128)S(1)}, f32[2,8,128]{2,1,0:T(8,128)S(1)}, u32[]{:S(2)}, u32[]{:S(2)}) collective-permute-start(f32[2,8,128]{2,1,0:T(8,128)S(1)} %get-tuple-element.13), channel_id=1, source_target_pairs={{0,4},{4,8},{8,12},{12,16},{16,20},{20,24},{24,28},{28,32},{32,36}... | collective-permute-start | bytes 24584 | tf_op jit(solution)/shard_map/ppermute | solution.py:329
  16.7 3.4 %collective-permute-start.1 = (f32[2,8,128]{2,1,0:T(8,128)S(1)}, f32[2,8,128]{2,1,0:T(8,128)S(1)}, u32[]{:S(2)}, u32[]{:S(2)}) collective-permute-start(f32[2,8,128]{2,1,0:T(8,128)S(1)} %get-tuple-element.14), channel_id=1, source_target_pairs={{4,0},{8,4},{12,8},{16,12},{20,16},{24,20},{28,24},{32,28},{36,32}... | collective-permute-start | bytes 24584 | tf_op jit(solution)/shard_map/ppermute | solution.py:329
  20.2 4.8 %collective-permute-start.2 = (f32[40,128]{1,0:T(8,128)S(1)}, f32[40,128]{1,0:T(8,128)S(1)}, u32[]{:S(2)}, u32[]{:S(2)}) collective-permute-start(f32[40,128]{1,0:T(8,128)S(1)} %get-tuple-element.16), channel_id=1, source_target_pairs={{0,1},{1,2},{2,3},{3,0},{4,5},{5,6},{6,7},{7,4},{8,9},{9,10},{10,1... | collective-permute-start | bytes 61448 | tf_op jit(solution)/shard_map/ppermute | solution.py:329
  22.1 3.0 %collective-permute-start.3 = (f32[40,128]{1,0:T(8,128)S(1)}, f32[40,128]{1,0:T(8,128)S(1)}, u32[]{:S(2)}, u32[]{:S(2)}) collective-permute-start(f32[40,128]{1,0:T(8,128)S(1)} %get-tuple-element.17), channel_id=1, source_target_pairs={{1,0},{2,1},{3,2},{0,3},{5,4},{6,5},{7,6},{4,7},{9,8},{10,9},{11,1... | collective-permute-start | bytes 61448 | tf_op jit(solution)/shard_map/ppermute | solution.py:329
  25.6 4.9 %collective-permute-start.4 = (bf16[64,16,256]{2,1,0:T(8,128)(2,1)S(1)}, bf16[64,16,256]{2,1,0:T(8,128)(2,1)S(1)}, u32[]{:S(2)}, u32[]{:S(2)}) collective-permute-start(bf16[64,16,256]{2,1,0:T(8,128)(2,1)S(1)} %all-to-all-done.near_ref), channel_id=1, source_target_pairs={{0,4},{4,0},{1,5},{5,1},{2,6},{6,2},{3,7},{7,3},{8,12},{12,8},{9,1... | collective-permute-start | bytes 1572872 | tf_op jit(solution)/shard_map/ppermute | solution.py:358

commit v4 on v3

--- a/solution.py
+++ b/solution.py
@@ -16,6 +16,7 @@
 COURANT = 0.05
 F32 = jnp.float32
 BF16 = jnp.bfloat16
+UNR = 15
 VMEM_LIMIT = 16 << 20
 
 
@@ -171,23 +172,57 @@
     field_ref[...] = f - COURANT * (wind_x * slope_x + wind_y * slope_y)
 
 
-def lstm_kernel(
-    near_ref, far_ref, field_ref, *refs
+def pick_owner(table_ref, pick, wanted, surf):
+    peers, features, slot_count = table_ref.shape
+    lane = lax.broadcasted_iota(jnp.int32, surf.shape, 1)
+    for k in range(0, peers, 16):
+        found = lax.dot_general(
+            pick,
+            table_ref[k : k + 16].reshape(16 * features, slot_count),
+            (((1,), (1,)), ((), ())),
+            preferred_element_type=F32,
+        )
+        for half in range(2):
+            own = wanted == lane // features + (k + 8 * half)
+            surf = jnp.where(own, found[:, half * LANES : (half + 1) * LANES], surf)
+    return surf
+
+
+def prepare_kernel(
+    near_ref, slots_hbm, state_w_hbm, surf_w_hbm, hidden_w_hbm, bias_hbm,
+    hidden_w_ref, in_w_ref, surf_ref, pick_ref, wanted_ref,
+    slots_ref, state_w_ref, surf_w_ref, bias_ref, arrived,
 ):
-    kept, out_ref = refs[:6], refs[6]
-    slots_ref, state_w_ref, surf_w_ref, hidden_w_ref, bias_ref, out_w_ref = refs[7:13]
-    in_w_ref, cell_ref, part_ref, pend_ref, past_ref, arrived = refs[13:]
-    copies = [
-        pltpu.make_async_copy(source, target, arrived.at[i])
-        for i, (source, target) in enumerate(zip(kept, refs[7:13]))
-    ]
+    pairs = (
+        (slots_hbm, slots_ref),
+        (state_w_hbm, state_w_ref),
+        (surf_w_hbm, surf_w_ref),
+        (bias_hbm, bias_ref),
+        (hidden_w_hbm, hidden_w_ref),
+    )
+    copies = [pltpu.make_async_copy(a, b, arrived.at[i]) for i, (a, b) in enumerate(pairs)]
     for copy in copies:
         copy.start()
-    rows = field_ref.shape[0]
-    gates = 4 * HID
-    unit = HID // 2
-    for i in (1, 2, 4):
-        copies[i].wait()
+    rows = surf_ref.shape[0]
+    copies[0].wait()
+    slots = slots_ref[...]
+    slots = jnp.concatenate(
+        [jnp.broadcast_to(slots[:, x : x + 1], (8, 2 * LANES)) for x in range(rows // 8)], axis=0
+    )
+    place = jnp.bitwise_and(slots, 255)
+    owner = lax.shift_right_logical(slots[:, :LANES], 8)
+    index = jnp.bitwise_or(
+        lax.shift_left(lax.shift_right_logical(owner, 3), 2), jnp.bitwise_and(owner, 3)
+    )
+    here = jnp.bitwise_and(lax.shift_right_logical(owner, 2), 1) == lax.axis_index("c")
+    pick = (lax.broadcasted_iota(jnp.int32, place.shape, 1) == place).astype(BF16)
+    pick_ref[...] = pick
+    wanted_ref[...] = jnp.where(here, -1, index)
+    surf_ref[...] = pick_owner(
+        near_ref, pick, jnp.where(here, index, -1), jnp.zeros((rows, LANES), F32)
+    )
+    for copy in copies[1:4]:
+        copy.wait()
     row = lax.broadcasted_iota(jnp.int32, (64, NV), 0)
     col = lax.broadcasted_iota(jnp.int32, (64, NV), 1)
     spread = (row % NV == col).astype(BF16)
@@ -201,31 +236,24 @@
     parts = jnp.where(r == 0, high, jnp.where(r == 1, mid, jnp.where(r == 2, low, 0.0)))
     in_w_ref[64:80] = parts.astype(BF16)
     in_w_ref[80:96] = surf_w_ref[...]
-    in_w_ref[96:128] = jnp.zeros((32, gates), BF16)
-
-    feature_lane = lax.broadcasted_iota(jnp.int32, (16, LANES), 1)
-    core = jnp.bitwise_and(lax.axis_index("c"), 1)
-    copies[0].wait()
-
-    def fetch(c, acc):
-        slot = slots_ref[jnp.bitwise_and(c, 7), lax.shift_right_logical(c, 3)]
-        owner = lax.shift_right_logical(slot, 8)
-        place = jnp.bitwise_and(slot, 255)
-        half = pl.multiple_of(jnp.bitwise_and(place, 128), 128)
-        index = jnp.bitwise_or(
-            lax.shift_left(lax.shift_right_logical(owner, 3), 2), jnp.bitwise_and(owner, 3)
-        )
-        here = jnp.bitwise_and(lax.shift_right_logical(owner, 2), 1) == core
-        near = near_ref[index, :, pl.ds(half, LANES)]
-        far = far_ref[index, :, pl.ds(half, LANES)]
-        tile = jnp.where(here, near, far).astype(F32)
-        shift = jnp.bitwise_and(c - place + 256, 127)
-        return jnp.where(feature_lane == c, pltpu.roll(tile, shift, 1), acc)
-
-    surf = lax.fori_loop(0, rows, fetch, jnp.zeros((16, LANES), F32), unroll=8)
-    surf = jnp.concatenate(
-        [jnp.zeros((80, LANES), F32), surf, jnp.zeros((32, LANES), F32)], axis=0
-    ).T
+    in_w_ref[96:128] = jnp.zeros((32, 4 * HID), BF16)
+    copies[4].wait()
+
+
+def lstm_kernel(
+    far_ref, field_ref, hidden_w_ref, in_w_ref, surf_ref, pick_ref, wanted_ref, out_w_hbm,
+    out_ref, out_w_ref, cell_ref, part_ref, pend_ref, past_ref, feed_ref, arrived,
+):
+    copy = pltpu.make_async_copy(out_w_hbm, out_w_ref, arrived)
+    copy.start()
+    rows = field_ref.shape[0]
+    features = far_ref.shape[1]
+    unit = HID // 2
+    surf = pick_owner(far_ref, pick_ref[...], wanted_ref[...], surf_ref[...])
+    row = lax.broadcasted_iota(jnp.int32, (LANES, LANES), 0)
+    col = lax.broadcasted_iota(jnp.int32, (LANES, LANES), 1)
+    fold = (col - 80 == row % features).astype(BF16)
+    surf = jnp.dot(surf.astype(BF16), fold, preferred_element_type=F32)
     lane = lax.broadcasted_iota(jnp.int32, (rows, LANES), 1)
     fixed = jnp.where((lane >= 64) & (lane < 67), 0.5, 0.5 * surf)
     field = field_ref[...]
@@ -261,11 +289,21 @@
         past_ref[level] = jnp.concatenate([low_half, high_half], axis=1)
         return high_half
 
-    def step(level, low_half):
-        x = level_input(level)
+    def feed(level):
+        x = jnp.concatenate([level_input(level), level_input(level + 1)], axis=0)
         for j in range(2):
             for q in range(4):
-                part_ref[j, q] = dot(x, in_w_ref[:, cols(q, j)]) + dot(
+                feed_ref[j, q] = dot(x, in_w_ref[:, cols(q, j)])
+
+    def two_steps(pair, low_half):
+        level = 2 * pair + 1
+        feed(level)
+        return step(level + 1, 1, step(level, 0, low_half))
+
+    def step(level, odd, low_half):
+        for j in range(2):
+            for q in range(4):
+                part_ref[j, q] = feed_ref[j, q, odd * rows : (odd + 1) * rows] + dot(
                     low_half, hidden_w_ref[0:unit, cols(q, j)]
                 )
         high_half = finish(level - 1, low_half)
@@ -277,23 +315,23 @@
             pend_ref[q] = part_ref[1, q] + dot(high_half, hidden_w_ref[unit:HID, cols(q, 1)])
         return new
 
-    copies[3].wait()
-    low_half = lax.fori_loop(1, LEVELS, step, low_half, unroll=4)
+    low_half = lax.fori_loop(0, LEVELS // 2 - 1, two_steps, low_half, unroll=UNR)
+    feed(LEVELS - 1)
+    low_half = step(LEVELS - 1, 0, low_half)
     finish(LEVELS - 1, low_half)
-    copies[5].wait()
-    row = lax.broadcasted_iota(jnp.int32, (NV, LANES), 0)
-    col = lax.broadcasted_iota(jnp.int32, (NV, LANES), 1)
-    spread = (col % NV == row).astype(BF16)
-    out_w = lax.dot_general(
-        out_w_ref[...], spread, (((0,), (0,)), ((), ())), preferred_element_type=F32
-    )
-    out_w = (out_w + out_w).astype(BF16)
-    group = 8
-    gain = jnp.zeros((rows, LANES), F32)
-    for k in range(LEVELS // group):
-        p = dot(past_ref[k * group : (k + 1) * group].reshape(group * rows, HID), out_w)
-        for i in range(group):
-            gain = jnp.where(lane // NV == k * group + i, p[i * rows : (i + 1) * rows], gain)
+    copy.wait()
+    out_w = out_w_ref[...].astype(F32)
+    out_w = jnp.concatenate([out_w + out_w, jnp.zeros((4, HID), F32)], axis=0).astype(BF16)
+    gain = []
+    for k in range(0, LEVELS, 8):
+        p = lax.dot_general(
+            out_w,
+            past_ref[k : k + 8].reshape(8 * rows, HID),
+            (((1,), (1,)), ((), ())),
+            preferred_element_type=F32,
+        )
+        gain += [p[0:NV, i * rows : (i + 1) * rows] for i in range(8)]
+    gain = jnp.concatenate(gain, axis=0).T
     out_ref[...] = field + gain.astype(BF16).astype(F32)
 
 
@@ -356,23 +394,39 @@
     field = call(third_kernel, block, g, before, after, left, right)
     near, _ = lax.optimization_barrier((near, field))
     far = lax.ppermute(near, "c", [(0, 1), (1, 0)])
-    kept = (assignment.T, w_state, w_surf, w_hidden, bias.reshape(1, 4 * HID), w_out.T)
+    kept = (assignment.T, w_state, w_surf, w_hidden, bias.reshape(1, 4 * HID))
+    prepared = call(
+        prepare_kernel,
+        (
+            like(HID, 4 * HID, dtype=BF16),
+            like(LANES, 4 * HID, dtype=BF16),
+            like(columns_here, LANES),
+            like(columns_here, slot_count, dtype=BF16),
+            like(columns_here, LANES, dtype=jnp.int32),
+        ),
+        near,
+        kept=kept,
+        scratch=(
+            *[pltpu.VMEM(a.shape, a.dtype) for i, a in enumerate(kept) if i != 3],
+            pltpu.SemaphoreType.DMA((len(kept),)),
+        ),
+        cost=pl.CostEstimate(flops=1 << 28, bytes_accessed=4 << 20, transcendentals=0),
+    )
     result = call(
         lstm_kernel,
         like(columns_here, channels),
-        near,
         far,
         field.reshape(columns_here, channels),
-        kept=kept,
+        *prepared,
+        kept=(w_out.T,),
         scratch=(
-            pltpu.SMEM(kept[0].shape, kept[0].dtype),
-            *[pltpu.VMEM(a.shape, a.dtype) for a in kept[1:]],
-            pltpu.VMEM((LANES, 4 * HID), BF16),
+            pltpu.VMEM((NV, HID), BF16),
             pltpu.VMEM((columns_here, HID), F32),
             pltpu.VMEM((2, 4, columns_here, HID // 2), F32),
             pltpu.VMEM((4, columns_here, HID // 2), F32),
             pltpu.VMEM((LEVELS, columns_here, HID), BF16),
-            pltpu.SemaphoreType.DMA((len(kept),)),
+            pltpu.VMEM((2, 4, 2 * columns_here, HID // 2), F32),
+            pltpu.SemaphoreType.DMA(()),
         ),
     )
     return result.reshape(node_rows, node_cols, channels)

time: 52.9 us -> 48.7 us (0.921)
  Pallas kernels: 24.9 us -> 21.8 us
  waiting for transfers between devices: 6.71 us -> 5.17 us
    pallas_call x5 -> x6, Pallas kernels: 24.9 us -> 21.8 us  [call(): pl.pallas_call(kernel, out_shape=out_shape, in_specs=[pl.BlockSpec(memory...]
    ppermute x1, waiting for transfers between devices: 1.54 us -> 0.01 us  [shards(): far = lax.ppermute(near, 'c', [(0, 1), (1, 0)])]
  transfers between devices with their start and end apart: 6 -> 6, of which waited for: 5 -> 4; matrix products, arithmetic and copies ran while one was open for 0% -> 0% of each run, Pallas kernels for 2% -> 6%
where the time goes in v4:
time: 48.7 us; the launch traced here: 48.4 us
  Pallas kernels  21.8 us (45%)
  starting transfers between devices  21.2 us (44%)
  waiting for transfers between devices  5.17 us (11%)
    pallas_call x6, Pallas kernels, call(): pl.pallas_call(kernel, out_shape=out_shape, in_specs=[pl.BlockSpec(memory...  21.8 us
    all_to_all x1, starting transfers between devices, shards(): lax.all_to_all(spread, ('z', 'y', 'x'), split_axis=0, concat_axis=0, tile...  12 us
    ppermute x2, starting transfers between devices, exchange(): lax.ppermute(to_upper, axes, up)  4.02 us
    ppermute x1, starting transfers between devices, shards(): far = lax.ppermute(near, 'c', [(0, 1), (1, 0)])  3.53 us
    ppermute x2, waiting for transfers between devices, exchange(): lax.ppermute(to_lower, axes, down)  2.65 us
    ppermute x2, waiting for transfers between devices, exchange(): lax.ppermute(to_upper, axes, up)  2.17 us
    ppermute x2, starting transfers between devices, exchange(): lax.ppermute(to_lower, axes, down)  1.63 us
  transfers between devices with their start and end apart: 6, of which 4 were waited for; matrix products, arithmetic and copies ran while one was open for 0% of the time, Pallas kernels for 6%

profile of v4, /device:TPU:1, one launch (start us, length us, event | category | flops | bytes accessed | tf_op | source)
XLA Modules:
  0.0 48.4 jit_solution(9284592560863275148)
XLA Ops:
  0.0 1.5 %shard_map.82 = bf16[64,16,256]{2,1,0:T(8,128)(2,1)} custom-call(bf16[16,256]{1,0:T(8,128)(2,1)} %bitcast.7), custom_call_target="tpu_custom_call" | custom-call | tf_op jit(solution)/shard_map/pallas_call | solution.py:341
  1.5 12.0 %all-to-all-start = ((bf16[64,16,256]{2,1,0:T(8,128)(2,1)}), bf16[64,16,256]{2,1,0:T(8,128)(2,1)S(1)}, u32[]{:S(2)}, u32[]{:S(2)}) async-start(bf16[64,16,256]{2,1,0:T(8,128)(2,1)} %shard_map.82), calls=%async_computation | async-start | bytes 1048576 | tf_op jit(solution)/shard_map/all_to_all | solution.py:390
  13.5 1.0 %shard_map.83 = (f32[16,8,128]{2,1,0:T(8,128)S(1)}, f32[2,8,128]{2,1,0:T(8,128)S(1)}, f32[2,8,128]{2,1,0:T(8,128)S(1)}) custom-call(f32[16,8,128]{2,1,0:T(8,128)} %state_ref.1), custom_call_target="tpu_custom_call" | custom-call | tf_op jit(solution)/shard_map/pallas_call | solution.py:341
  14.5 2.2 %collective-permute-start = (f32[2,8,128]{2,1,0:T(8,128)S(1)}, f32[2,8,128]{2,1,0:T(8,128)S(1)}, u32[]{:S(2)}, u32[]{:S(2)}) collective-permute-start(f32[2,8,128]{2,1,0:T(8,128)S(1)} %get-tuple-element.18), channel_id=1, source_target_pairs={{0,4},{4,8},{8,12},{12,16},{16,20},{20,24},{24,28},{28,32},{32,36}... | collective-permute-start | bytes 24584 | tf_op jit(solution)/shard_map/ppermute | solution.py:367
  16.7 0.0 collective-permute-start.1
  16.7 0.8 %collective-permute-done.before_ref = f32[2,8,128]{2,1,0:T(8,128)S(1)} collective-permute-done((f32[2,8,128]{2,1,0:T(8,128)S(1)}, f32[2,8,128]{2,1,0:T(8,128)S(1)}, u32[]{:S(2)}, u32[]{:S(2)}) %collective-permute-start) | collective-permute-done | bytes 8224 | tf_op jit(solution)/shard_map/ppermute | solution.py:367
  17.5 2.6 %collective-permute-done.1.after_ref = f32[2,8,128]{2,1,0:T(8,128)S(1)} collective-permute-done((f32[2,8,128]{2,1,0:T(8,128)S(1)}, f32[2,8,128]{2,1,0:T(8,128)S(1)}, u32[]{:S(2)}, u32[]{:S(2)}) %collective-permute-start.1) | collective-permute-done | bytes 8224 | tf_op jit(solution)/shard_map/ppermute | solution.py:367
  20.2 0.1 shard_map.84
  20.2 1.8 %collective-permute-start.2 = (f32[40,128]{1,0:T(8,128)S(1)}, f32[40,128]{1,0:T(8,128)S(1)}, u32[]{:S(2)}, u32[]{:S(2)}) collective-permute-start(f32[40,128]{1,0:T(8,128)S(1)} %get-tuple-element.21), channel_id=1, source_target_pairs={{0,1},{1,2},{2,3},{3,0},{4,5},{5,6},{6,7},{7,4},{8,9},{9,10},{10,1... | collective-permute-start | bytes 61448 | tf_op jit(solution)/shard_map/ppermute | solution.py:367
  22.0 1.6 %collective-permute-start.3 = (f32[40,128]{1,0:T(8,128)S(1)}, f32[40,128]{1,0:T(8,128)S(1)}, u32[]{:S(2)}, u32[]{:S(2)}) collective-permute-start(f32[40,128]{1,0:T(8,128)S(1)} %get-tuple-element.22), channel_id=1, source_target_pairs={{1,0},{2,1},{3,2},{0,3},{5,4},{6,5},{7,6},{4,7},{9,8},{10,9},{11,1... | collective-permute-start | bytes 61448 | tf_op jit(solution)/shard_map/ppermute | solution.py:367
  23.7 1.4 %collective-permute-done.2.left_ref = f32[40,128]{1,0:T(8,128)S(1)} collective-permute-done((f32[40,128]{1,0:T(8,128)S(1)}, f32[40,128]{1,0:T(8,128)S(1)}, u32[]{:S(2)}, u32[]{:S(2)}) %collective-permute-start.2) | collective-permute-done | bytes 20512 | tf_op jit(solution)/shard_map/ppermute | solution.py:367
  25.1 0.0 collective-permute-done.3.right_ref
  25.1 0.2 shard_map.85
  25.3 0.3 all-to-all-done.near_ref
  25.6 3.5 %collective-permute-start.4 = (bf16[64,16,256]{2,1,0:T(8,128)(2,1)S(1)}, bf16[64,16,256]{2,1,0:T(8,128)(2,1)S(1)}, u32[]{:S(2)}, u32[]{:S(2)}) collective-permute-start(bf16[64,16,256]{2,1,0:T(8,128)(2,1)S(1)} %all-to-all-done.near_ref), channel_id=1, source_target_pairs={{0,4},{4,0},{1,5},{5,1},{2,6},{6,2},{3,7},{7,3},{8,12},{12,8},{9,1... | collective-permute-start | bytes 1572872 | tf_op jit(solution)/shard_map/ppermute | solution.py:396
  29.1 1.7 %shard_map.86 = (bf16[512,2048]{1,0:T(8,128)(2,1)S(1)}, bf16[128,2048]{1,0:T(8,128)(2,1)S(1)}, f32[128,128]{1,0:T(8,128)S(1)}, bf16[128,256]{1,0:T(8,128)(2,1)S(1)}, s32[128,128]{1,0:T(8,128)S(1)}) custom-call(bf16[64,16,256]{2,1,0:T(8,128)(2,1)S(1)} %all-to-all-done.near_ref, s32[8,16]{1,0:T(8,128)} %bitcast.9, bf16[4,2048]{1,0:T(4,128)(2,1)} %state_w_hbm.1, ...), custom_call_target="tpu_custom_call" | custom-call | flops 268435456 | bytes 4194304 | tf_op jit(solution)/shard_map/pallas_call | solution.py:341
  30.9 0.0 collective-permute-done.4.far_ref
  30.9 17.3 %shard_map.87 = f32[128,128]{1,0:T(8,128)} custom-call(bf16[64,16,256]{2,1,0:T(8,128)(2,1)S(1)} %collective-permute-done.4.far_ref, f32[128,128]{1,0:T(8,128)S(1)} %bitcast.6, bf16[512,2048]{1,0:T(8,128)(2,1)S(1)} %get-tuple-element.24.hidden_w_ref, bf16[128,2048]{1,0:T(8,128)(2,1)S(1)} %get-tuple-element.25.in_w_ref, ...), custom_call_target="tpu_custom_call" | custom-call | tf_op jit(solution)/shard_map/pallas_call | solution.py:341
Async XLA Ops:
  1.5 24.1 %all-to-all-start = ((bf16[64,16,256]{2,1,0:T(8,128)(2,1)}), bf16[64,16,256]{2,1,0:T(8,128)(2,1)S(1)}, u32[]{:S(2)}, u32[]{:S(2)}) async-start(bf16[64,16,256]{2,1,0:T(8,128)(2,1)} %shard_map.82), calls=%async_computation | async-start | bytes 1048576 | tf_op jit(solution)/shard_map/all_to_all | solution.py:390
  14.5 3.0 %collective-permute-start = (f32[2,8,128]{2,1,0:T(8,128)S(1)}, f32[2,8,128]{2,1,0:T(8,128)S(1)}, u32[]{:S(2)}, u32[]{:S(2)}) collective-permute-start(f32[2,8,128]{2,1,0:T(8,128)S(1)} %get-tuple-element.18), channel_id=1, source_target_pairs={{0,4},{4,8},{8,12},{12,16},{16,20},{20,24},{24,28},{28,32},{32,36}... | collective-permute-start | bytes 24584 | tf_op jit(solution)/shard_map/ppermute | solution.py:367
  16.7 3.4 %collective-permute-start.1 = (f32[2,8,128]{2,1,0:T(8,128)S(1)}, f32[2,8,128]{2,1,0:T(8,128)S(1)}, u32[]{:S(2)}, u32[]{:S(2)}) collective-permute-start(f32[2,8,128]{2,1,0:T(8,128)S(1)} %get-tuple-element.19), channel_id=1, source_target_pairs={{4,0},{8,4},{12,8},{16,12},{20,16},{24,20},{28,24},{32,28},{36,32}... | collective-permute-start | bytes 24584 | tf_op jit(solution)/shard_map/ppermute | solution.py:367
  20.2 4.8 %collective-permute-start.2 = (f32[40,128]{1,0:T(8,128)S(1)}, f32[40,128]{1,0:T(8,128)S(1)}, u32[]{:S(2)}, u32[]{:S(2)}) collective-permute-start(f32[40,128]{1,0:T(8,128)S(1)} %get-tuple-element.21), channel_id=1, source_target_pairs={{0,1},{1,2},{2,3},{3,0},{4,5},{5,6},{6,7},{7,4},{8,9},{9,10},{10,1... | collective-permute-start | bytes 61448 | tf_op jit(solution)/shard_map/ppermute | solution.py:367
  22.0 3.0 %collective-permute-start.3 = (f32[40,128]{1,0:T(8,128)S(1)}, f32[40,128]{1,0:T(8,128)S(1)}, u32[]{:S(2)}, u32[]{:S(2)}) collective-permute-start(f32[40,128]{1,0:T(8,128)S(1)} %get-tuple-element.22), channel_id=1, source_target_pairs={{1,0},{2,1},{3,2},{0,3},{5,4},{6,5},{7,6},{4,7},{9,8},{10,9},{11,1... | collective-permute-start | bytes 61448 | tf_op jit(solution)/shard_map/ppermute | solution.py:367
  25.6 5.3 %collective-permute-start.4 = (bf16[64,16,256]{2,1,0:T(8,128)(2,1)S(1)}, bf16[64,16,256]{2,1,0:T(8,128)(2,1)S(1)}, u32[]{:S(2)}, u32[]{:S(2)}) collective-permute-start(bf16[64,16,256]{2,1,0:T(8,128)(2,1)S(1)} %all-to-all-done.near_ref), channel_id=1, source_target_pairs={{0,4},{4,0},{1,5},{5,1},{2,6},{6,2},{3,7},{7,3},{8,12},{12,8},{9,1... | collective-permute-start | bytes 1572872 | tf_op jit(solution)/shard_map/ppermute | solution.py:396

commit v5 on v4

--- a/solution.py
+++ b/solution.py
@@ -107,32 +107,41 @@
     return jnp.stack(pieces, axis=0)
 
 
-def spread_kernel(surface_ref, spread_ref, here_ref, arrived):
-    copy = pltpu.make_async_copy(surface_ref, here_ref, arrived)
-    copy.start()
-    copy.wait()
-    spread_ref[...] = jnp.broadcast_to(here_ref[...][None], spread_ref.shape)
-
-
-def first_kernel(state_ref, moved_ref, to_before_ref, to_after_ref, here_ref, arrived):
-    copy = pltpu.make_async_copy(state_ref, here_ref, arrived)
-    copy.start()
-    copy.wait()
-    f = here_ref[...]
+def first_kernel(
+    state_hbm, surface_hbm, moved_ref, to_core_ref, to_chip_ref, spread_ref, state_ref, surface_ref, arrived
+):
+    copies = (
+        pltpu.make_async_copy(surface_hbm, surface_ref, arrived.at[0]),
+        pltpu.make_async_copy(state_hbm, state_ref, arrived.at[1]),
+    )
+    for copy in copies:
+        copy.start()
+    copies[0].wait()
+    spread_ref[...] = jnp.broadcast_to(surface_ref[...][None], spread_ref.shape)
+    copies[1].wait()
+    f = state_ref[...]
     wind_x, wind_y = winds(f)
     a = f - COURANT * (wind_x * along_x(f) + wind_y * along_y(f))
     moved_ref[...] = a
     n = a.shape[0]
-    to_before_ref[0] = a[0]
-    to_before_ref[1] = D[0][1] * a[1] + D[0][2] * a[2] + D[0][3] * ((a[3] + a[4]) * 0.5)
-    to_after_ref[0] = a[n - 1]
-    to_after_ref[1] = (
-        D[3][0] * ((a[n - 4] + a[n - 5]) * 0.5) + D[3][1] * a[n - 3] + D[3][2] * a[n - 2]
-    )
-
-
-def second_kernel(moved_ref, before_ref, after_ref, g_ref, to_left_ref, to_right_ref):
-    g = average_x(moved_ref[...], before_ref[0], after_ref[0])
+    first = D[0][1] * a[1] + D[0][2] * a[2] + D[0][3] * ((a[3] + a[4]) * 0.5)
+    last = D[3][0] * ((a[n - 4] + a[n - 5]) * 0.5) + D[3][1] * a[n - 3] + D[3][2] * a[n - 2]
+    even = lax.axis_index("c") == 0
+    to_core_ref[0] = jnp.where(even, a[n - 1], a[0])
+    to_core_ref[1] = jnp.where(even, last, first)
+    to_chip_ref[0] = jnp.where(even, a[0], a[n - 1])
+    to_chip_ref[1] = jnp.where(even, first, last)
+
+
+def sort_edges(core_ref, chip_ref):
+    even = lax.axis_index("c") == 0
+    core, chip = core_ref[...], chip_ref[...]
+    return jnp.where(even, chip, core), jnp.where(even, core, chip)
+
+
+def second_kernel(moved_ref, core_ref, chip_ref, g_ref, to_left_ref, to_right_ref):
+    before, after = sort_edges(core_ref, chip_ref)
+    g = average_x(moved_ref[...], before[0], after[0])
     g_ref[...] = g
     rows, size, _ = g.shape
     middle = (g[:, 3] + g[:, 4]) * 0.5
@@ -142,7 +151,7 @@
     to_right_ref[rows : 2 * rows] = (
         D[3][0] * middle + D[3][1] * g[:, size - 3] + D[3][2] * g[:, size - 2]
     )
-    up, down = before_ref[1], after_ref[1]
+    up, down = before[1], after[1]
     y = lax.broadcasted_iota(jnp.int32, (size, LANES), 0)
     to_left_ref[2 * rows : 2 * rows + 8] = jnp.where(
         y == 0, up, jnp.where(y == 1, pltpu.roll(down, 1, 0), 0.0)
@@ -152,7 +161,8 @@
     )
 
 
-def third_kernel(g_ref, before_ref, after_ref, left_ref, right_ref, field_ref):
+def third_kernel(g_ref, core_ref, chip_ref, left_ref, right_ref, field_ref):
+    before, after = sort_edges(core_ref, chip_ref)
     g = g_ref[...]
     rows, size, _ = g.shape
     left_g = left_ref[0:rows].reshape(rows, 1, LANES)
@@ -160,8 +170,8 @@
     f = average_y(g, left_g, right_g)
     tail_l = left_ref[2 * rows : 2 * rows + 8]
     tail_r = right_ref[2 * rows : 2 * rows + 8]
-    up = average_y(before_ref[1:2], tail_l[0:1].reshape(1, 1, LANES), tail_r[0:1].reshape(1, 1, LANES))[0]
-    down = average_y(after_ref[1:2], tail_l[1:2].reshape(1, 1, LANES), tail_r[1:2].reshape(1, 1, LANES))[0]
+    up = average_y(before[1:2], tail_l[0:1].reshape(1, 1, LANES), tail_r[0:1].reshape(1, 1, LANES))[0]
+    down = average_y(after[1:2], tail_l[1:2].reshape(1, 1, LANES), tail_r[1:2].reshape(1, 1, LANES))[0]
     slope_x = average_x(
         along_x(f), D[3][3] * f[0] + up, D[0][0] * f[rows - 1] + down
     )
@@ -374,24 +384,31 @@
     peers = lax.axis_size("z") * lax.axis_size("y") * lax.axis_size("x")
     block = like(node_rows, node_cols, channels)
     edge = like(2, node_cols, channels)
-    spread = call(
-        spread_kernel,
-        like(peers, features, slot_count, dtype=BF16),
-        kept=(surface.T,),
-        scratch=(pltpu.VMEM((features, slot_count), BF16), pltpu.SemaphoreType.DMA(())),
-    )
-    moved, to_before, to_after = call(
+    moved, to_core, to_chip, spread = call(
         first_kernel,
-        (block, edge, edge),
-        kept=(state,),
-        scratch=(pltpu.VMEM(state.shape, F32), pltpu.SemaphoreType.DMA(())),
-    )
-    before, after = exchange(to_before, to_after, ELEM)
+        (block, edge, edge, like(peers, features, slot_count, dtype=BF16)),
+        kept=(state, surface.T),
+        scratch=(
+            pltpu.VMEM(state.shape, F32),
+            pltpu.VMEM((features, slot_count), BF16),
+            pltpu.SemaphoreType.DMA((2,)),
+        ),
+    )
+    core = lax.ppermute(to_core, "c", [(0, 1), (1, 0)])
+    count = math.prod(lax.axis_size(a) for a in ELEM)
+    pairs = [(i, (i + 1) % count) for i in range(1, count, 2)]
+    chip = lax.ppermute(to_chip, ELEM, pairs + [(j, i) for i, j in pairs])
     near = lax.all_to_all(spread, ("z", "y", "x"), split_axis=0, concat_axis=0, tiled=True)
     side = like(2 * node_rows + 8, channels)
-    g, to_left, to_right = call(second_kernel, (block, side, side), moved, before, after)
+    g, to_left, to_right = call(
+        second_kernel,
+        (block, side, side),
+        moved,
+        core,
+        chip,
+    )
     left, right = exchange(to_left, to_right, ("x",))
-    field = call(third_kernel, block, g, before, after, left, right)
+    field = call(third_kernel, block, g, core, chip, left, right)
     near, _ = lax.optimization_barrier((near, field))
     far = lax.ppermute(near, "c", [(0, 1), (1, 0)])
     kept = (assignment.T, w_state, w_surf, w_hidden, bias.reshape(1, 4 * HID))

time: 48.7 us -> 47.6 us (0.977)
  Pallas kernels: 21.8 us -> 21 us
    ppermute x0 -> x2, waiting for transfers between devices: none -> 3.14 us  [the longest x1 3.14 us: shards(): chip = lax.ppermute(to_chip, ELEM, pairs + [(j, i) for i, j in pairs])]
    ppermute x2 -> x1, waiting for transfers between devices: 2.65 us -> 0.01 us  [exchange(): lax.ppermute(to_lower, axes, down)]
    ppermute x0 -> x2, starting transfers between devices: none -> 2.3 us  [the longest x1 1.27 us: shards(): chip = lax.ppermute(to_chip, ELEM, pairs + [(j, i) for i, j in pairs])]
    ppermute x2 -> x1, starting transfers between devices: 4.02 us -> 1.77 us  [exchange(): lax.ppermute(to_upper, axes, up)]
    ppermute x1, starting transfers between devices: 3.53 us -> 2.23 us  [shards(): far = lax.ppermute(near, 'c', [(0, 1), (1, 0)])]
    ppermute x2 -> x1, starting transfers between devices: 1.63 us -> 2.88 us  [exchange(): lax.ppermute(to_lower, axes, down)]
    pallas_call x6 -> x5, Pallas kernels: 21.8 us -> 21 us  [call(): pl.pallas_call(kernel, out_shape=out_shape, in_specs=[pl.BlockSpec(memory...]
    ppermute x2 -> x1, waiting for transfers between devices: 2.17 us -> 1.38 us  [exchange(): lax.ppermute(to_upper, axes, up)]
  transfers between devices with their start and end apart: 6 -> 6, of which waited for: 4 -> 3; matrix products, arithmetic and copies ran while one was open for 0% -> 0% of each run, Pallas kernels for 6% -> 4%
where the time goes in v5:
time: 47.6 us; the launch traced here: 47.2 us
  starting transfers between devices  21.2 us (45%)
  Pallas kernels  21 us (44%)
  waiting for transfers between devices  4.88 us (10%)
    pallas_call x5, Pallas kernels, call(): pl.pallas_call(kernel, out_shape=out_shape, in_specs=[pl.BlockSpec(memory...  21 us
    all_to_all x1, starting transfers between devices, shards(): lax.all_to_all(spread, ('z', 'y', 'x'), split_axis=0, concat_axis=0, tile...  12 us
    ppermute x1, waiting for transfers between devices, shards(): chip = lax.ppermute(to_chip, ELEM, pairs + [(j, i) for i, j in pairs])  3.14 us
    ppermute x1, starting transfers between devices, exchange(): lax.ppermute(to_lower, axes, down)  2.88 us
    ppermute x1, starting transfers between devices, shards(): far = lax.ppermute(near, 'c', [(0, 1), (1, 0)])  2.23 us
    ppermute x1, starting transfers between devices, exchange(): lax.ppermute(to_upper, axes, up)  1.77 us
    ppermute x1, waiting for transfers between devices, exchange(): lax.ppermute(to_upper, axes, up)  1.38 us
    ppermute x1, starting transfers between devices, shards(): chip = lax.ppermute(to_chip, ELEM, pairs + [(j, i) for i, j in pairs])  1.27 us
  transfers between devices with their start and end apart: 6, of which 3 were waited for; matrix products, arithmetic and copies ran while one was open for 0% of the time, Pallas kernels for 4%

profile of v5, /device:TPU:1, one launch (start us, length us, event | category | flops | bytes accessed | tf_op | source)
XLA Modules:
  0.0 47.2 jit_solution(14537806479735746535)
XLA Ops:
  0.0 1.7 %shard_map.82 = (f32[16,8,128]{2,1,0:T(8,128)S(1)}, f32[2,8,128]{2,1,0:T(8,128)S(1)}, f32[2,8,128]{2,1,0:T(8,128)S(1)}, bf16[64,16,256]{2,1,0:T(8,128)(2,1)}) custom-call(f32[16,8,128]{2,1,0:T(8,128)} %state_hbm.1, bf16[16,256]{1,0:T(8,128)(2,1)} %bitcast.8), custom_call_target="tpu_custom_call" | custom-call | tf_op jit(solution)/shard_map/pallas_call | solution.py:351
  1.7 12.0 %all-to-all-start = ((bf16[64,16,256]{2,1,0:T(8,128)(2,1)}), bf16[64,16,256]{2,1,0:T(8,128)(2,1)S(1)}, u32[]{:S(2)}, u32[]{:S(2)}) async-start(bf16[64,16,256]{2,1,0:T(8,128)(2,1)} %get-tuple-element.18), calls=%async_computation | async-start | bytes 1048576 | tf_op jit(solution)/shard_map/all_to_all | solution.py:401
  13.7 1.0 %collective-permute-start = (f32[2,8,128]{2,1,0:T(8,128)S(1)}, f32[2,8,128]{2,1,0:T(8,128)S(1)}, u32[]{:S(2)}, u32[]{:S(2)}) collective-permute-start(f32[2,8,128]{2,1,0:T(8,128)S(1)} %get-tuple-element.20), channel_id=1, source_target_pairs={{0,4},{4,0},{1,5},{5,1},{2,6},{6,2},{3,7},{7,3},{8,12},{12,8},{9,1... | collective-permute-start | bytes 24584 | tf_op jit(solution)/shard_map/ppermute | solution.py:397
  14.7 1.3 %collective-permute-start.1 = (f32[2,8,128]{2,1,0:T(8,128)S(1)}, f32[2,8,128]{2,1,0:T(8,128)S(1)}, u32[]{:S(2)}, u32[]{:S(2)}) collective-permute-start(f32[2,8,128]{2,1,0:T(8,128)S(1)} %get-tuple-element.21), channel_id=1, source_target_pairs={{4,8},{12,16},{20,24},{28,32},{36,40},{44,48},{52,56},{60,64},{68,... | collective-permute-start | bytes 24584 | tf_op jit(solution)/shard_map/ppermute | solution.py:400
  16.0 0.0 collective-permute-done.core_ref
  16.0 3.1 %collective-permute-done.1.chip_ref = f32[2,8,128]{2,1,0:T(8,128)S(1)} collective-permute-done((f32[2,8,128]{2,1,0:T(8,128)S(1)}, f32[2,8,128]{2,1,0:T(8,128)S(1)}, u32[]{:S(2)}, u32[]{:S(2)}) %collective-permute-start.1) | collective-permute-done | bytes 8224 | tf_op jit(solution)/shard_map/ppermute | solution.py:400
  19.1 0.1 shard_map.83
  19.2 1.8 %collective-permute-start.2 = (f32[40,128]{1,0:T(8,128)S(1)}, f32[40,128]{1,0:T(8,128)S(1)}, u32[]{:S(2)}, u32[]{:S(2)}) collective-permute-start(f32[40,128]{1,0:T(8,128)S(1)} %get-tuple-element.23), channel_id=1, source_target_pairs={{0,1},{1,2},{2,3},{3,0},{4,5},{5,6},{6,7},{7,4},{8,9},{9,10},{10,1... | collective-permute-start | bytes 61448 | tf_op jit(solution)/shard_map/ppermute | solution.py:377
  20.9 2.9 %collective-permute-start.3 = (f32[40,128]{1,0:T(8,128)S(1)}, f32[40,128]{1,0:T(8,128)S(1)}, u32[]{:S(2)}, u32[]{:S(2)}) collective-permute-start(f32[40,128]{1,0:T(8,128)S(1)} %get-tuple-element.24), channel_id=1, source_target_pairs={{1,0},{2,1},{3,2},{0,3},{5,4},{6,5},{7,6},{4,7},{9,8},{10,9},{11,1... | collective-permute-start | bytes 61448 | tf_op jit(solution)/shard_map/ppermute | solution.py:377
  23.8 1.4 %collective-permute-done.2.left_ref = f32[40,128]{1,0:T(8,128)S(1)} collective-permute-done((f32[40,128]{1,0:T(8,128)S(1)}, f32[40,128]{1,0:T(8,128)S(1)}, u32[]{:S(2)}, u32[]{:S(2)}) %collective-permute-start.2) | collective-permute-done | bytes 20512 | tf_op jit(solution)/shard_map/ppermute | solution.py:377
  25.2 0.0 collective-permute-done.3.right_ref
  25.2 0.2 shard_map.84
  25.4 0.3 all-to-all-done.near_ref
  25.8 2.2 %collective-permute-start.4 = (bf16[64,16,256]{2,1,0:T(8,128)(2,1)S(1)}, bf16[64,16,256]{2,1,0:T(8,128)(2,1)S(1)}, u32[]{:S(2)}, u32[]{:S(2)}) collective-permute-start(bf16[64,16,256]{2,1,0:T(8,128)(2,1)S(1)} %all-to-all-done.near_ref), channel_id=1, source_target_pairs={{0,4},{4,0},{1,5},{5,1},{2,6},{6,2},{3,7},{7,3},{8,12},{12,8},{9,1... | collective-permute-start | bytes 1572872 | tf_op jit(solution)/shard_map/ppermute | solution.py:413
  28.0 1.7 %shard_map.85 = (bf16[512,2048]{1,0:T(8,128)(2,1)S(1)}, bf16[128,2048]{1,0:T(8,128)(2,1)S(1)}, f32[128,128]{1,0:T(8,128)S(1)}, bf16[128,256]{1,0:T(8,128)(2,1)S(1)}, s32[128,128]{1,0:T(8,128)S(1)}) custom-call(bf16[64,16,256]{2,1,0:T(8,128)(2,1)S(1)} %all-to-all-done.near_ref, s32[8,16]{1,0:T(8,128)} %bitcast.9, bf16[4,2048]{1,0:T(4,128)(2,1)} %state_w_hbm.1, ...), custom_call_target="tpu_custom_call" | custom-call | flops 268435456 | bytes 4194304 | tf_op jit(solution)/shard_map/pallas_call | solution.py:351
  29.7 0.0 collective-permute-done.4.far_ref
  29.7 17.3 %shard_map.86 = f32[128,128]{1,0:T(8,128)} custom-call(bf16[64,16,256]{2,1,0:T(8,128)(2,1)S(1)} %collective-permute-done.4.far_ref, f32[128,128]{1,0:T(8,128)S(1)} %bitcast.6, bf16[512,2048]{1,0:T(8,128)(2,1)S(1)} %get-tuple-element.26.hidden_w_ref, bf16[128,2048]{1,0:T(8,128)(2,1)S(1)} %get-tuple-element.27.in_w_ref, ...), custom_call_target="tpu_custom_call" | custom-call | tf_op jit(solution)/shard_map/pallas_call | solution.py:351
Async XLA Ops:
  1.7 24.1 %all-to-all-start = ((bf16[64,16,256]{2,1,0:T(8,128)(2,1)}), bf16[64,16,256]{2,1,0:T(8,128)(2,1)S(1)}, u32[]{:S(2)}, u32[]{:S(2)}) async-start(bf16[64,16,256]{2,1,0:T(8,128)(2,1)} %get-tuple-element.18), calls=%async_computation | async-start | bytes 1048576 | tf_op jit(solution)/shard_map/all_to_all | solution.py:401
  13.7 2.3 %collective-permute-start = (f32[2,8,128]{2,1,0:T(8,128)S(1)}, f32[2,8,128]{2,1,0:T(8,128)S(1)}, u32[]{:S(2)}, u32[]{:S(2)}) collective-permute-start(f32[2,8,128]{2,1,0:T(8,128)S(1)} %get-tuple-element.20), channel_id=1, source_target_pairs={{0,4},{4,0},{1,5},{5,1},{2,6},{6,2},{3,7},{7,3},{8,12},{12,8},{9,1... | collective-permute-start | bytes 24584 | tf_op jit(solution)/shard_map/ppermute | solution.py:397
  14.7 4.4 %collective-permute-start.1 = (f32[2,8,128]{2,1,0:T(8,128)S(1)}, f32[2,8,128]{2,1,0:T(8,128)S(1)}, u32[]{:S(2)}, u32[]{:S(2)}) collective-permute-start(f32[2,8,128]{2,1,0:T(8,128)S(1)} %get-tuple-element.21), channel_id=1, source_target_pairs={{4,8},{12,16},{20,24},{28,32},{36,40},{44,48},{52,56},{60,64},{68,... | collective-permute-start | bytes 24584 | tf_op jit(solution)/shard_map/ppermute | solution.py:400
  19.2 6.0 %collective-permute-start.2 = (f32[40,128]{1,0:T(8,128)S(1)}, f32[40,128]{1,0:T(8,128)S(1)}, u32[]{:S(2)}, u32[]{:S(2)}) collective-permute-start(f32[40,128]{1,0:T(8,128)S(1)} %get-tuple-element.23), channel_id=1, source_target_pairs={{0,1},{1,2},{2,3},{3,0},{4,5},{5,6},{6,7},{7,4},{8,9},{9,10},{10,1... | collective-permute-start | bytes 61448 | tf_op jit(solution)/shard_map/ppermute | solution.py:377
  20.9 4.3 %collective-permute-start.3 = (f32[40,128]{1,0:T(8,128)S(1)}, f32[40,128]{1,0:T(8,128)S(1)}, u32[]{:S(2)}, u32[]{:S(2)}) collective-permute-start(f32[40,128]{1,0:T(8,128)S(1)} %get-tuple-element.24), channel_id=1, source_target_pairs={{1,0},{2,1},{3,2},{0,3},{5,4},{6,5},{7,6},{4,7},{9,8},{10,9},{11,1... | collective-permute-start | bytes 61448 | tf_op jit(solution)/shard_map/ppermute | solution.py:377
  25.8 4.0 %collective-permute-start.4 = (bf16[64,16,256]{2,1,0:T(8,128)(2,1)S(1)}, bf16[64,16,256]{2,1,0:T(8,128)(2,1)S(1)}, u32[]{:S(2)}, u32[]{:S(2)}) collective-permute-start(bf16[64,16,256]{2,1,0:T(8,128)(2,1)S(1)} %all-to-all-done.near_ref), channel_id=1, source_target_pairs={{0,4},{4,0},{1,5},{5,1},{2,6},{6,2},{3,7},{7,3},{8,12},{12,8},{9,1... | collective-permute-start | bytes 1572872 | tf_op jit(solution)/shard_map/ppermute | solution.py:413

commit v6 on v5

--- a/solution.py
+++ b/solution.py
@@ -16,7 +16,6 @@
 COURANT = 0.05
 F32 = jnp.float32
 BF16 = jnp.bfloat16
-UNR = 15
 VMEM_LIMIT = 16 << 20
 
 
@@ -299,23 +298,14 @@
         past_ref[level] = jnp.concatenate([low_half, high_half], axis=1)
         return high_half
 
-    def feed(level):
-        x = jnp.concatenate([level_input(level), level_input(level + 1)], axis=0)
+    def step(level, low_half):
+        x = level_input(level)
         for j in range(2):
             for q in range(4):
                 feed_ref[j, q] = dot(x, in_w_ref[:, cols(q, j)])
-
-    def two_steps(pair, low_half):
-        level = 2 * pair + 1
-        feed(level)
-        return step(level + 1, 1, step(level, 0, low_half))
-
-    def step(level, odd, low_half):
         for j in range(2):
             for q in range(4):
-                part_ref[j, q] = feed_ref[j, q, odd * rows : (odd + 1) * rows] + dot(
-                    low_half, hidden_w_ref[0:unit, cols(q, j)]
-                )
+                part_ref[j, q] = feed_ref[j, q] + dot(low_half, hidden_w_ref[0:unit, cols(q, j)])
         high_half = finish(level - 1, low_half)
         g = [
             part_ref[0, q] + dot(high_half, hidden_w_ref[unit:HID, cols(q, 0)]) for q in range(4)
@@ -325,9 +315,7 @@
             pend_ref[q] = part_ref[1, q] + dot(high_half, hidden_w_ref[unit:HID, cols(q, 1)])
         return new
 
-    low_half = lax.fori_loop(0, LEVELS // 2 - 1, two_steps, low_half, unroll=UNR)
-    feed(LEVELS - 1)
-    low_half = step(LEVELS - 1, 0, low_half)
+    low_half = lax.fori_loop(1, LEVELS, step, low_half, unroll=LEVELS - 1)
     finish(LEVELS - 1, low_half)
     copy.wait()
     out_w = out_w_ref[...].astype(F32)
@@ -442,7 +430,7 @@
             pltpu.VMEM((2, 4, columns_here, HID // 2), F32),
             pltpu.VMEM((4, columns_here, HID // 2), F32),
             pltpu.VMEM((LEVELS, columns_here, HID), BF16),
-            pltpu.VMEM((2, 4, 2 * columns_here, HID // 2), F32),
+            pltpu.VMEM((2, 4, columns_here, HID // 2), F32),
             pltpu.SemaphoreType.DMA(()),
         ),
     )

time: 47.6 us -> 46.5 us (0.977)
  Pallas kernels: 21 us -> 19.9 us
    pallas_call x5, Pallas kernels: 21 us -> 19.9 us  [call(): pl.pallas_call(kernel, out_shape=out_shape, in_specs=[pl.BlockSpec(memory...]
where the time goes in v6:
time: 46.5 us; the launch traced here: 46.2 us
  starting transfers between devices  21.2 us (46%)
  Pallas kernels  19.9 us (43%)
  waiting for transfers between devices  4.88 us (10%)
    pallas_call x5, Pallas kernels, call(): pl.pallas_call(kernel, out_shape=out_shape, in_specs=[pl.BlockSpec(memory...  19.9 us
    all_to_all x1, starting transfers between devices, shards(): lax.all_to_all(spread, ('z', 'y', 'x'), split_axis=0, concat_axis=0, tile...  12 us
    ppermute x1, waiting for transfers between devices, shards(): chip = lax.ppermute(to_chip, ELEM, pairs + [(j, i) for i, j in pairs])  3.14 us
    ppermute x1, starting transfers between devices, exchange(): lax.ppermute(to_lower, axes, down)  2.88 us
    ppermute x1, starting transfers between devices, shards(): far = lax.ppermute(near, 'c', [(0, 1), (1, 0)])  2.23 us
    ppermute x1, starting transfers between devices, exchange(): lax.ppermute(to_upper, axes, up)  1.77 us
    ppermute x1, waiting for transfers between devices, exchange(): lax.ppermute(to_upper, axes, up)  1.38 us
    ppermute x1, starting transfers between devices, shards(): chip = lax.ppermute(to_chip, ELEM, pairs + [(j, i) for i, j in pairs])  1.27 us
  transfers between devices with their start and end apart: 6, of which 3 were waited for; matrix products, arithmetic and copies ran while one was open for 0% of the time, Pallas kernels for 4%

profile of v6, /device:TPU:1, one launch (start us, length us, event | category | flops | bytes accessed | tf_op | source)
XLA Modules:
  0.0 46.2 jit_solution(16916790784700030219)
XLA Ops:
  0.0 1.7 %shard_map.82 = (f32[16,8,128]{2,1,0:T(8,128)S(1)}, f32[2,8,128]{2,1,0:T(8,128)S(1)}, f32[2,8,128]{2,1,0:T(8,128)S(1)}, bf16[64,16,256]{2,1,0:T(8,128)(2,1)}) custom-call(f32[16,8,128]{2,1,0:T(8,128)} %state_hbm.1, bf16[16,256]{1,0:T(8,128)(2,1)} %bitcast.8), custom_call_target="tpu_custom_call" | custom-call | tf_op jit(solution)/shard_map/pallas_call | solution.py:339
  1.7 12.0 %all-to-all-start = ((bf16[64,16,256]{2,1,0:T(8,128)(2,1)}), bf16[64,16,256]{2,1,0:T(8,128)(2,1)S(1)}, u32[]{:S(2)}, u32[]{:S(2)}) async-start(bf16[64,16,256]{2,1,0:T(8,128)(2,1)} %get-tuple-element.18), calls=%async_computation | async-start | bytes 1048576 | tf_op jit(solution)/shard_map/all_to_all | solution.py:389
  13.7 1.0 %collective-permute-start = (f32[2,8,128]{2,1,0:T(8,128)S(1)}, f32[2,8,128]{2,1,0:T(8,128)S(1)}, u32[]{:S(2)}, u32[]{:S(2)}) collective-permute-start(f32[2,8,128]{2,1,0:T(8,128)S(1)} %get-tuple-element.20), channel_id=1, source_target_pairs={{0,4},{4,0},{1,5},{5,1},{2,6},{6,2},{3,7},{7,3},{8,12},{12,8},{9,1... | collective-permute-start | bytes 24584 | tf_op jit(solution)/shard_map/ppermute | solution.py:385
  14.7 1.3 %collective-permute-start.1 = (f32[2,8,128]{2,1,0:T(8,128)S(1)}, f32[2,8,128]{2,1,0:T(8,128)S(1)}, u32[]{:S(2)}, u32[]{:S(2)}) collective-permute-start(f32[2,8,128]{2,1,0:T(8,128)S(1)} %get-tuple-element.21), channel_id=1, source_target_pairs={{4,8},{12,16},{20,24},{28,32},{36,40},{44,48},{52,56},{60,64},{68,... | collective-permute-start | bytes 24584 | tf_op jit(solution)/shard_map/ppermute | solution.py:388
  16.0 0.0 collective-permute-done.core_ref
  16.0 3.1 %collective-permute-done.1.chip_ref = f32[2,8,128]{2,1,0:T(8,128)S(1)} collective-permute-done((f32[2,8,128]{2,1,0:T(8,128)S(1)}, f32[2,8,128]{2,1,0:T(8,128)S(1)}, u32[]{:S(2)}, u32[]{:S(2)}) %collective-permute-start.1) | collective-permute-done | bytes 8224 | tf_op jit(solution)/shard_map/ppermute | solution.py:388
  19.1 0.1 shard_map.83
  19.2 1.8 %collective-permute-start.2 = (f32[40,128]{1,0:T(8,128)S(1)}, f32[40,128]{1,0:T(8,128)S(1)}, u32[]{:S(2)}, u32[]{:S(2)}) collective-permute-start(f32[40,128]{1,0:T(8,128)S(1)} %get-tuple-element.23), channel_id=1, source_target_pairs={{0,1},{1,2},{2,3},{3,0},{4,5},{5,6},{6,7},{7,4},{8,9},{9,10},{10,1... | collective-permute-start | bytes 61448 | tf_op jit(solution)/shard_map/ppermute | solution.py:365
  20.9 2.9 %collective-permute-start.3 = (f32[40,128]{1,0:T(8,128)S(1)}, f32[40,128]{1,0:T(8,128)S(1)}, u32[]{:S(2)}, u32[]{:S(2)}) collective-permute-start(f32[40,128]{1,0:T(8,128)S(1)} %get-tuple-element.24), channel_id=1, source_target_pairs={{1,0},{2,1},{3,2},{0,3},{5,4},{6,5},{7,6},{4,7},{9,8},{10,9},{11,1... | collective-permute-start | bytes 61448 | tf_op jit(solution)/shard_map/ppermute | solution.py:365
  23.8 1.4 %collective-permute-done.2.left_ref = f32[40,128]{1,0:T(8,128)S(1)} collective-permute-done((f32[40,128]{1,0:T(8,128)S(1)}, f32[40,128]{1,0:T(8,128)S(1)}, u32[]{:S(2)}, u32[]{:S(2)}) %collective-permute-start.2) | collective-permute-done | bytes 20512 | tf_op jit(solution)/shard_map/ppermute | solution.py:365
  25.2 0.0 collective-permute-done.3.right_ref
  25.2 0.2 shard_map.84
  25.4 0.3 all-to-all-done.near_ref
  25.8 2.2 %collective-permute-start.4 = (bf16[64,16,256]{2,1,0:T(8,128)(2,1)S(1)}, bf16[64,16,256]{2,1,0:T(8,128)(2,1)S(1)}, u32[]{:S(2)}, u32[]{:S(2)}) collective-permute-start(bf16[64,16,256]{2,1,0:T(8,128)(2,1)S(1)} %all-to-all-done.near_ref), channel_id=1, source_target_pairs={{0,4},{4,0},{1,5},{5,1},{2,6},{6,2},{3,7},{7,3},{8,12},{12,8},{9,1... | collective-permute-start | bytes 1572872 | tf_op jit(solution)/shard_map/ppermute | solution.py:401
  28.0 1.7 %shard_map.85 = (bf16[512,2048]{1,0:T(8,128)(2,1)S(1)}, bf16[128,2048]{1,0:T(8,128)(2,1)S(1)}, f32[128,128]{1,0:T(8,128)S(1)}, bf16[128,256]{1,0:T(8,128)(2,1)S(1)}, s32[128,128]{1,0:T(8,128)S(1)}) custom-call(bf16[64,16,256]{2,1,0:T(8,128)(2,1)S(1)} %all-to-all-done.near_ref, s32[8,16]{1,0:T(8,128)} %bitcast.9, bf16[4,2048]{1,0:T(4,128)(2,1)} %state_w_hbm.1, ...), custom_call_target="tpu_custom_call" | custom-call | flops 268435456 | bytes 4194304 | tf_op jit(solution)/shard_map/pallas_call | solution.py:339
  29.7 0.0 collective-permute-done.4.far_ref
  29.7 16.3 %shard_map.86 = f32[128,128]{1,0:T(8,128)} custom-call(bf16[64,16,256]{2,1,0:T(8,128)(2,1)S(1)} %collective-permute-done.4.far_ref, f32[128,128]{1,0:T(8,128)S(1)} %bitcast.6, bf16[512,2048]{1,0:T(8,128)(2,1)S(1)} %get-tuple-element.26.hidden_w_ref, bf16[128,2048]{1,0:T(8,128)(2,1)S(1)} %get-tuple-element.27.in_w_ref, ...), custom_call_target="tpu_custom_call" | custom-call | tf_op jit(solution)/shard_map/pallas_call | solution.py:339
Async XLA Ops:
  1.7 24.1 %all-to-all-start = ((bf16[64,16,256]{2,1,0:T(8,128)(2,1)}), bf16[64,16,256]{2,1,0:T(8,128)(2,1)S(1)}, u32[]{:S(2)}, u32[]{:S(2)}) async-start(bf16[64,16,256]{2,1,0:T(8,128)(2,1)} %get-tuple-element.18), calls=%async_computation | async-start | bytes 1048576 | tf_op jit(solution)/shard_map/all_to_all | solution.py:389
  13.7 2.3 %collective-permute-start = (f32[2,8,128]{2,1,0:T(8,128)S(1)}, f32[2,8,128]{2,1,0:T(8,128)S(1)}, u32[]{:S(2)}, u32[]{:S(2)}) collective-permute-start(f32[2,8,128]{2,1,0:T(8,128)S(1)} %get-tuple-element.20), channel_id=1, source_target_pairs={{0,4},{4,0},{1,5},{5,1},{2,6},{6,2},{3,7},{7,3},{8,12},{12,8},{9,1... | collective-permute-start | bytes 24584 | tf_op jit(solution)/shard_map/ppermute | solution.py:385
  14.7 4.4 %collective-permute-start.1 = (f32[2,8,128]{2,1,0:T(8,128)S(1)}, f32[2,8,128]{2,1,0:T(8,128)S(1)}, u32[]{:S(2)}, u32[]{:S(2)}) collective-permute-start(f32[2,8,128]{2,1,0:T(8,128)S(1)} %get-tuple-element.21), channel_id=1, source_target_pairs={{4,8},{12,16},{20,24},{28,32},{36,40},{44,48},{52,56},{60,64},{68,... | collective-permute-start | bytes 24584 | tf_op jit(solution)/shard_map/ppermute | solution.py:388
  19.2 6.0 %collective-permute-start.2 = (f32[40,128]{1,0:T(8,128)S(1)}, f32[40,128]{1,0:T(8,128)S(1)}, u32[]{:S(2)}, u32[]{:S(2)}) collective-permute-start(f32[40,128]{1,0:T(8,128)S(1)} %get-tuple-element.23), channel_id=1, source_target_pairs={{0,1},{1,2},{2,3},{3,0},{4,5},{5,6},{6,7},{7,4},{8,9},{9,10},{10,1... | collective-permute-start | bytes 61448 | tf_op jit(solution)/shard_map/ppermute | solution.py:365
  20.9 4.3 %collective-permute-start.3 = (f32[40,128]{1,0:T(8,128)S(1)}, f32[40,128]{1,0:T(8,128)S(1)}, u32[]{:S(2)}, u32[]{:S(2)}) collective-permute-start(f32[40,128]{1,0:T(8,128)S(1)} %get-tuple-element.24), channel_id=1, source_target_pairs={{1,0},{2,1},{3,2},{0,3},{5,4},{6,5},{7,6},{4,7},{9,8},{10,9},{11,1... | collective-permute-start | bytes 61448 | tf_op jit(solution)/shard_map/ppermute | solution.py:365
  25.8 4.0 %collective-permute-start.4 = (bf16[64,16,256]{2,1,0:T(8,128)(2,1)S(1)}, bf16[64,16,256]{2,1,0:T(8,128)(2,1)S(1)}, u32[]{:S(2)}, u32[]{:S(2)}) collective-permute-start(bf16[64,16,256]{2,1,0:T(8,128)(2,1)S(1)} %all-to-all-done.near_ref), channel_id=1, source_target_pairs={{0,4},{4,0},{1,5},{5,1},{2,6},{6,2},{3,7},{7,3},{8,12},{12,8},{9,1... | collective-permute-start | bytes 1572872 | tf_op jit(solution)/shard_map/ppermute | solution.py:401

commit v7 on v6

--- a/solution.py
+++ b/solution.py
@@ -16,6 +16,7 @@
 COURANT = 0.05
 F32 = jnp.float32
 BF16 = jnp.bfloat16
+GROUP = 8
 VMEM_LIMIT = 16 << 20
 
 
@@ -315,20 +316,26 @@
             pend_ref[q] = part_ref[1, q] + dot(high_half, hidden_w_ref[unit:HID, cols(q, 1)])
         return new
 
-    low_half = lax.fori_loop(1, LEVELS, step, low_half, unroll=LEVELS - 1)
-    finish(LEVELS - 1, low_half)
     copy.wait()
     out_w = out_w_ref[...].astype(F32)
     out_w = jnp.concatenate([out_w + out_w, jnp.zeros((4, HID), F32)], axis=0).astype(BF16)
-    gain = []
-    for k in range(0, LEVELS, 8):
+
+    def gains(first, count):
         p = lax.dot_general(
             out_w,
-            past_ref[k : k + 8].reshape(8 * rows, HID),
+            past_ref[first : first + count].reshape(count * rows, HID),
             (((1,), (1,)), ((), ())),
             preferred_element_type=F32,
         )
-        gain += [p[0:NV, i * rows : (i + 1) * rows] for i in range(8)]
+        return [p[0:NV, i * rows : (i + 1) * rows] for i in range(count)]
+
+    gain = []
+    for level in range(1, LEVELS):
+        low_half = step(level, low_half)
+        if level % GROUP == 1 and level > GROUP:
+            gain += gains(level - 1 - GROUP, GROUP)
+    finish(LEVELS - 1, low_half)
+    gain += gains(LEVELS - GROUP, GROUP)
     gain = jnp.concatenate(gain, axis=0).T
     out_ref[...] = field + gain.astype(BF16).astype(F32)
 

time: 46.5 us -> 46.1 us (level)
  no operation moved by 1% of the time
where the time goes in v7:
time: 46.1 us; the launch traced here: 45.8 us
  starting transfers between devices  21.2 us (46%)
  Pallas kernels  19.5 us (42%)
  waiting for transfers between devices  4.88 us (11%)
    pallas_call x5, Pallas kernels, call(): pl.pallas_call(kernel, out_shape=out_shape, in_specs=[pl.BlockSpec(memory...  19.5 us
    all_to_all x1, starting transfers between devices, shards(): lax.all_to_all(spread, ('z', 'y', 'x'), split_axis=0, concat_axis=0, tile...  12 us
    ppermute x1, waiting for transfers between devices, shards(): chip = lax.ppermute(to_chip, ELEM, pairs + [(j, i) for i, j in pairs])  3.14 us
    ppermute x1, starting transfers between devices, exchange(): lax.ppermute(to_lower, axes, down)  2.88 us
    ppermute x1, starting transfers between devices, shards(): far = lax.ppermute(near, 'c', [(0, 1), (1, 0)])  2.23 us
    ppermute x1, starting transfers between devices, exchange(): lax.ppermute(to_upper, axes, up)  1.77 us
    ppermute x1, waiting for transfers between devices, exchange(): lax.ppermute(to_upper, axes, up)  1.38 us
    ppermute x1, starting transfers between devices, shards(): chip = lax.ppermute(to_chip, ELEM, pairs + [(j, i) for i, j in pairs])  1.27 us
  transfers between devices with their start and end apart: 6, of which 3 were waited for; matrix products, arithmetic and copies ran while one was open for 0% of the time, Pallas kernels for 4%

profile of v7, /device:TPU:1, one launch (start us, length us, event | category | flops | bytes accessed | tf_op | source)
XLA Modules:
  0.0 45.8 jit_solution(11705900047696012333)
XLA Ops:
  0.0 1.7 %shard_map.82 = (f32[16,8,128]{2,1,0:T(8,128)S(1)}, f32[2,8,128]{2,1,0:T(8,128)S(1)}, f32[2,8,128]{2,1,0:T(8,128)S(1)}, bf16[64,16,256]{2,1,0:T(8,128)(2,1)}) custom-call(f32[16,8,128]{2,1,0:T(8,128)} %state_hbm.1, bf16[16,256]{1,0:T(8,128)(2,1)} %bitcast.8), custom_call_target="tpu_custom_call" | custom-call | tf_op jit(solution)/shard_map/pallas_call | solution.py:346
  1.7 12.0 %all-to-all-start = ((bf16[64,16,256]{2,1,0:T(8,128)(2,1)}), bf16[64,16,256]{2,1,0:T(8,128)(2,1)S(1)}, u32[]{:S(2)}, u32[]{:S(2)}) async-start(bf16[64,16,256]{2,1,0:T(8,128)(2,1)} %get-tuple-element.18), calls=%async_computation | async-start | bytes 1048576 | tf_op jit(solution)/shard_map/all_to_all | solution.py:396
  13.7 1.0 %collective-permute-start = (f32[2,8,128]{2,1,0:T(8,128)S(1)}, f32[2,8,128]{2,1,0:T(8,128)S(1)}, u32[]{:S(2)}, u32[]{:S(2)}) collective-permute-start(f32[2,8,128]{2,1,0:T(8,128)S(1)} %get-tuple-element.20), channel_id=1, source_target_pairs={{0,4},{4,0},{1,5},{5,1},{2,6},{6,2},{3,7},{7,3},{8,12},{12,8},{9,1... | collective-permute-start | bytes 24584 | tf_op jit(solution)/shard_map/ppermute | solution.py:392
  14.7 1.3 %collective-permute-start.1 = (f32[2,8,128]{2,1,0:T(8,128)S(1)}, f32[2,8,128]{2,1,0:T(8,128)S(1)}, u32[]{:S(2)}, u32[]{:S(2)}) collective-permute-start(f32[2,8,128]{2,1,0:T(8,128)S(1)} %get-tuple-element.21), channel_id=1, source_target_pairs={{4,8},{12,16},{20,24},{28,32},{36,40},{44,48},{52,56},{60,64},{68,... | collective-permute-start | bytes 24584 | tf_op jit(solution)/shard_map/ppermute | solution.py:395
  16.0 0.0 collective-permute-done.core_ref
  16.0 3.1 %collective-permute-done.1.chip_ref = f32[2,8,128]{2,1,0:T(8,128)S(1)} collective-permute-done((f32[2,8,128]{2,1,0:T(8,128)S(1)}, f32[2,8,128]{2,1,0:T(8,128)S(1)}, u32[]{:S(2)}, u32[]{:S(2)}) %collective-permute-start.1) | collective-permute-done | bytes 8224 | tf_op jit(solution)/shard_map/ppermute | solution.py:395
  19.1 0.1 shard_map.83
  19.2 1.8 %collective-permute-start.2 = (f32[40,128]{1,0:T(8,128)S(1)}, f32[40,128]{1,0:T(8,128)S(1)}, u32[]{:S(2)}, u32[]{:S(2)}) collective-permute-start(f32[40,128]{1,0:T(8,128)S(1)} %get-tuple-element.23), channel_id=1, source_target_pairs={{0,1},{1,2},{2,3},{3,0},{4,5},{5,6},{6,7},{7,4},{8,9},{9,10},{10,1... | collective-permute-start | bytes 61448 | tf_op jit(solution)/shard_map/ppermute | solution.py:372
  20.9 2.9 %collective-permute-start.3 = (f32[40,128]{1,0:T(8,128)S(1)}, f32[40,128]{1,0:T(8,128)S(1)}, u32[]{:S(2)}, u32[]{:S(2)}) collective-permute-start(f32[40,128]{1,0:T(8,128)S(1)} %get-tuple-element.24), channel_id=1, source_target_pairs={{1,0},{2,1},{3,2},{0,3},{5,4},{6,5},{7,6},{4,7},{9,8},{10,9},{11,1... | collective-permute-start | bytes 61448 | tf_op jit(solution)/shard_map/ppermute | solution.py:372
  23.8 1.4 %collective-permute-done.2.left_ref = f32[40,128]{1,0:T(8,128)S(1)} collective-permute-done((f32[40,128]{1,0:T(8,128)S(1)}, f32[40,128]{1,0:T(8,128)S(1)}, u32[]{:S(2)}, u32[]{:S(2)}) %collective-permute-start.2) | collective-permute-done | bytes 20512 | tf_op jit(solution)/shard_map/ppermute | solution.py:372
  25.2 0.0 collective-permute-done.3.right_ref
  25.2 0.2 shard_map.84
  25.4 0.3 all-to-all-done.near_ref
  25.8 2.2 %collective-permute-start.4 = (bf16[64,16,256]{2,1,0:T(8,128)(2,1)S(1)}, bf16[64,16,256]{2,1,0:T(8,128)(2,1)S(1)}, u32[]{:S(2)}, u32[]{:S(2)}) collective-permute-start(bf16[64,16,256]{2,1,0:T(8,128)(2,1)S(1)} %all-to-all-done.near_ref), channel_id=1, source_target_pairs={{0,4},{4,0},{1,5},{5,1},{2,6},{6,2},{3,7},{7,3},{8,12},{12,8},{9,1... | collective-permute-start | bytes 1572872 | tf_op jit(solution)/shard_map/ppermute | solution.py:408
  28.0 1.7 %shard_map.85 = (bf16[512,2048]{1,0:T(8,128)(2,1)S(1)}, bf16[128,2048]{1,0:T(8,128)(2,1)S(1)}, f32[128,128]{1,0:T(8,128)S(1)}, bf16[128,256]{1,0:T(8,128)(2,1)S(1)}, s32[128,128]{1,0:T(8,128)S(1)}) custom-call(bf16[64,16,256]{2,1,0:T(8,128)(2,1)S(1)} %all-to-all-done.near_ref, s32[8,16]{1,0:T(8,128)} %bitcast.9, bf16[4,2048]{1,0:T(4,128)(2,1)} %state_w_hbm.1, ...), custom_call_target="tpu_custom_call" | custom-call | flops 268435456 | bytes 4194304 | tf_op jit(solution)/shard_map/pallas_call | solution.py:346
  29.7 0.0 collective-permute-done.4.far_ref
  29.7 15.9 %shard_map.86 = f32[128,128]{1,0:T(8,128)} custom-call(bf16[64,16,256]{2,1,0:T(8,128)(2,1)S(1)} %collective-permute-done.4.far_ref, f32[128,128]{1,0:T(8,128)S(1)} %bitcast.6, bf16[512,2048]{1,0:T(8,128)(2,1)S(1)} %get-tuple-element.26.hidden_w_ref, bf16[128,2048]{1,0:T(8,128)(2,1)S(1)} %get-tuple-element.27.in_w_ref, ...), custom_call_target="tpu_custom_call" | custom-call | tf_op jit(solution)/shard_map/pallas_call | solution.py:346
Async XLA Ops:
  1.7 24.1 %all-to-all-start = ((bf16[64,16,256]{2,1,0:T(8,128)(2,1)}), bf16[64,16,256]{2,1,0:T(8,128)(2,1)S(1)}, u32[]{:S(2)}, u32[]{:S(2)}) async-start(bf16[64,16,256]{2,1,0:T(8,128)(2,1)} %get-tuple-element.18), calls=%async_computation | async-start | bytes 1048576 | tf_op jit(solution)/shard_map/all_to_all | solution.py:396
  13.7 2.3 %collective-permute-start = (f32[2,8,128]{2,1,0:T(8,128)S(1)}, f32[2,8,128]{2,1,0:T(8,128)S(1)}, u32[]{:S(2)}, u32[]{:S(2)}) collective-permute-start(f32[2,8,128]{2,1,0:T(8,128)S(1)} %get-tuple-element.20), channel_id=1, source_target_pairs={{0,4},{4,0},{1,5},{5,1},{2,6},{6,2},{3,7},{7,3},{8,12},{12,8},{9,1... | collective-permute-start | bytes 24584 | tf_op jit(solution)/shard_map/ppermute | solution.py:392
  14.7 4.4 %collective-permute-start.1 = (f32[2,8,128]{2,1,0:T(8,128)S(1)}, f32[2,8,128]{2,1,0:T(8,128)S(1)}, u32[]{:S(2)}, u32[]{:S(2)}) collective-permute-start(f32[2,8,128]{2,1,0:T(8,128)S(1)} %get-tuple-element.21), channel_id=1, source_target_pairs={{4,8},{12,16},{20,24},{28,32},{36,40},{44,48},{52,56},{60,64},{68,... | collective-permute-start | bytes 24584 | tf_op jit(solution)/shard_map/ppermute | solution.py:395
  19.2 6.0 %collective-permute-start.2 = (f32[40,128]{1,0:T(8,128)S(1)}, f32[40,128]{1,0:T(8,128)S(1)}, u32[]{:S(2)}, u32[]{:S(2)}) collective-permute-start(f32[40,128]{1,0:T(8,128)S(1)} %get-tuple-element.23), channel_id=1, source_target_pairs={{0,1},{1,2},{2,3},{3,0},{4,5},{5,6},{6,7},{7,4},{8,9},{9,10},{10,1... | collective-permute-start | bytes 61448 | tf_op jit(solution)/shard_map/ppermute | solution.py:372
  20.9 4.3 %collective-permute-start.3 = (f32[40,128]{1,0:T(8,128)S(1)}, f32[40,128]{1,0:T(8,128)S(1)}, u32[]{:S(2)}, u32[]{:S(2)}) collective-permute-start(f32[40,128]{1,0:T(8,128)S(1)} %get-tuple-element.24), channel_id=1, source_target_pairs={{1,0},{2,1},{3,2},{0,3},{5,4},{6,5},{7,6},{4,7},{9,8},{10,9},{11,1... | collective-permute-start | bytes 61448 | tf_op jit(solution)/shard_map/ppermute | solution.py:372
  25.8 4.0 %collective-permute-start.4 = (bf16[64,16,256]{2,1,0:T(8,128)(2,1)S(1)}, bf16[64,16,256]{2,1,0:T(8,128)(2,1)S(1)}, u32[]{:S(2)}, u32[]{:S(2)}) collective-permute-start(bf16[64,16,256]{2,1,0:T(8,128)(2,1)S(1)} %all-to-all-done.near_ref), channel_id=1, source_target_pairs={{0,4},{4,0},{1,5},{5,1},{2,6},{6,2},{3,7},{7,3},{8,12},{12,8},{9,1... | collective-permute-start | bytes 1572872 | tf_op jit(solution)/shard_map/ppermute | solution.py:408

commit v8 on v7

--- a/solution.py
+++ b/solution.py
@@ -404,7 +404,7 @@
     )
     left, right = exchange(to_left, to_right, ("x",))
     field = call(third_kernel, block, g, core, chip, left, right)
-    near, _ = lax.optimization_barrier((near, field))
+    near, _ = lax.optimization_barrier((near, left))
     far = lax.ppermute(near, "c", [(0, 1), (1, 0)])
     kept = (assignment.T, w_state, w_surf, w_hidden, bias.reshape(1, 4 * HID))
     prepared = call(

time: 46.1 us -> 49.1 us (1.065)
  waiting for transfers between devices: 4.88 us -> 9.98 us
  starting transfers between devices: 21.2 us -> 18.9 us
    ppermute x1, waiting for transfers between devices: 1.38 us -> 4.26 us  [exchange(): lax.ppermute(to_upper, axes, up)]
    ppermute x1, starting transfers between devices: 2.88 us -> 0.62 us  [exchange(): lax.ppermute(to_lower, axes, down)]
    ppermute x1, waiting for transfers between devices: 0.01 us -> 2.02 us  [exchange(): lax.ppermute(to_lower, axes, down)]
  transfers between devices with their start and end apart: 6 -> 6, of which waited for: 3 -> 4; matrix products, arithmetic and copies ran while one was open for 0% -> 0% of each run, Pallas kernels for 4% -> 4%
where the time goes in v8:
time: 49.1 us; the launch traced here: 48.8 us
  Pallas kernels  19.7 us (40%)
  starting transfers between devices  18.9 us (38%)
  waiting for transfers between devices  9.98 us (20%)
    pallas_call x5, Pallas kernels, call(): pl.pallas_call(kernel, out_shape=out_shape, in_specs=[pl.BlockSpec(memory...  19.7 us
    all_to_all x1, starting transfers between devices, shards(): lax.all_to_all(spread, ('z', 'y', 'x'), split_axis=0, concat_axis=0, tile...  12 us
    ppermute x1, waiting for transfers between devices, exchange(): lax.ppermute(to_upper, axes, up)  4.26 us
    ppermute x1, waiting for transfers between devices, shards(): chip = lax.ppermute(to_chip, ELEM, pairs + [(j, i) for i, j in pairs])  3.14 us
    ppermute x1, starting transfers between devices, shards(): far = lax.ppermute(near, 'c', [(0, 1), (1, 0)])  2.23 us
    ppermute x1, waiting for transfers between devices, exchange(): lax.ppermute(to_lower, axes, down)  2.02 us
    ppermute x1, starting transfers between devices, exchange(): lax.ppermute(to_upper, axes, up)  1.77 us
    ppermute x1, starting transfers between devices, shards(): chip = lax.ppermute(to_chip, ELEM, pairs + [(j, i) for i, j in pairs])  1.27 us
  transfers between devices with their start and end apart: 6, of which 4 were waited for; matrix products, arithmetic and copies ran while one was open for 0% of the time, Pallas kernels for 4%

profile of v8, /device:TPU:1, one launch (start us, length us, event | category | flops | bytes accessed | tf_op | source)
XLA Modules:
  0.0 48.8 jit_solution(15929507389713761198)
XLA Ops:
  0.0 1.7 %shard_map.82 = (f32[16,8,128]{2,1,0:T(8,128)S(1)}, f32[2,8,128]{2,1,0:T(8,128)S(1)}, f32[2,8,128]{2,1,0:T(8,128)S(1)}, bf16[64,16,256]{2,1,0:T(8,128)(2,1)}) custom-call(f32[16,8,128]{2,1,0:T(8,128)} %state_hbm.1, bf16[16,256]{1,0:T(8,128)(2,1)} %bitcast.8), custom_call_target="tpu_custom_call" | custom-call | tf_op jit(solution)/shard_map/pallas_call | solution.py:346
  1.7 12.0 %all-to-all-start = ((bf16[64,16,256]{2,1,0:T(8,128)(2,1)}), bf16[64,16,256]{2,1,0:T(8,128)(2,1)S(1)}, u32[]{:S(2)}, u32[]{:S(2)}) async-start(bf16[64,16,256]{2,1,0:T(8,128)(2,1)} %get-tuple-element.18), calls=%async_computation | async-start | bytes 1048576 | tf_op jit(solution)/shard_map/all_to_all | solution.py:396
  13.7 1.0 %collective-permute-start = (f32[2,8,128]{2,1,0:T(8,128)S(1)}, f32[2,8,128]{2,1,0:T(8,128)S(1)}, u32[]{:S(2)}, u32[]{:S(2)}) collective-permute-start(f32[2,8,128]{2,1,0:T(8,128)S(1)} %get-tuple-element.20), channel_id=1, source_target_pairs={{0,4},{4,0},{1,5},{5,1},{2,6},{6,2},{3,7},{7,3},{8,12},{12,8},{9,1... | collective-permute-start | bytes 24584 | tf_op jit(solution)/shard_map/ppermute | solution.py:392
  14.7 1.3 %collective-permute-start.1 = (f32[2,8,128]{2,1,0:T(8,128)S(1)}, f32[2,8,128]{2,1,0:T(8,128)S(1)}, u32[]{:S(2)}, u32[]{:S(2)}) collective-permute-start(f32[2,8,128]{2,1,0:T(8,128)S(1)} %get-tuple-element.21), channel_id=1, source_target_pairs={{4,8},{12,16},{20,24},{28,32},{36,40},{44,48},{52,56},{60,64},{68,... | collective-permute-start | bytes 24584 | tf_op jit(solution)/shard_map/ppermute | solution.py:395
  16.0 0.0 collective-permute-done.core_ref
  16.0 3.1 %collective-permute-done.1.chip_ref = f32[2,8,128]{2,1,0:T(8,128)S(1)} collective-permute-done((f32[2,8,128]{2,1,0:T(8,128)S(1)}, f32[2,8,128]{2,1,0:T(8,128)S(1)}, u32[]{:S(2)}, u32[]{:S(2)}) %collective-permute-start.1) | collective-permute-done | bytes 8224 | tf_op jit(solution)/shard_map/ppermute | solution.py:395
  19.1 0.1 shard_map.83
  19.2 1.8 %collective-permute-start.2 = (f32[40,128]{1,0:T(8,128)S(1)}, f32[40,128]{1,0:T(8,128)S(1)}, u32[]{:S(2)}, u32[]{:S(2)}) collective-permute-start(f32[40,128]{1,0:T(8,128)S(1)} %get-tuple-element.22), channel_id=1, source_target_pairs={{0,1},{1,2},{2,3},{3,0},{4,5},{5,6},{6,7},{7,4},{8,9},{9,10},{10,1... | collective-permute-start | bytes 61448 | tf_op jit(solution)/shard_map/ppermute | solution.py:372
  20.9 4.3 %collective-permute-done.2.left_ref = f32[40,128]{1,0:T(8,128)S(1)} collective-permute-done((f32[40,128]{1,0:T(8,128)S(1)}, f32[40,128]{1,0:T(8,128)S(1)}, u32[]{:S(2)}, u32[]{:S(2)}) %collective-permute-start.2) | collective-permute-done | bytes 20512 | tf_op jit(solution)/shard_map/ppermute | solution.py:372
  25.2 0.6 %all-to-all-done.near_ref = bf16[64,16,256]{2,1,0:T(8,128)(2,1)S(1)} async-done(((bf16[64,16,256]{2,1,0:T(8,128)(2,1)}), bf16[64,16,256]{2,1,0:T(8,128)(2,1)S(1)}, u32[]{:S(2)}, u32[]{:S(2)}) %all-to-all-start) | async-done | bytes 524320 | tf_op jit(solution)/shard_map/all_to_all | solution.py:396
  25.8 2.2 %collective-permute-start.3 = (bf16[64,16,256]{2,1,0:T(8,128)(2,1)S(1)}, bf16[64,16,256]{2,1,0:T(8,128)(2,1)S(1)}, u32[]{:S(2)}, u32[]{:S(2)}) collective-permute-start(bf16[64,16,256]{2,1,0:T(8,128)(2,1)S(1)} %all-to-all-done.near_ref), channel_id=1, source_target_pairs={{0,4},{4,0},{1,5},{5,1},{2,6},{6,2},{3,7},{7,3},{8,12},{12,8},{9,1... | collective-permute-start | bytes 1572872 | tf_op jit(solution)/shard_map/ppermute | solution.py:408
  28.0 0.6 %collective-permute-start.4 = (f32[40,128]{1,0:T(8,128)S(1)}, f32[40,128]{1,0:T(8,128)S(1)}, u32[]{:S(2)}, u32[]{:S(2)}) collective-permute-start(f32[40,128]{1,0:T(8,128)S(1)} %get-tuple-element.25), channel_id=1, source_target_pairs={{1,0},{2,1},{3,2},{0,3},{5,4},{6,5},{7,6},{4,7},{9,8},{10,9},{11,1... | collective-permute-start | bytes 61448 | tf_op jit(solution)/shard_map/ppermute | solution.py:372
  28.6 2.0 %collective-permute-done.4.right_ref = f32[40,128]{1,0:T(8,128)S(1)} collective-permute-done((f32[40,128]{1,0:T(8,128)S(1)}, f32[40,128]{1,0:T(8,128)S(1)}, u32[]{:S(2)}, u32[]{:S(2)}) %collective-permute-start.4) | collective-permute-done | bytes 20512 | tf_op jit(solution)/shard_map/ppermute | solution.py:372
  30.6 0.2 shard_map.84
  30.8 1.7 %shard_map.85 = (bf16[512,2048]{1,0:T(8,128)(2,1)S(1)}, bf16[128,2048]{1,0:T(8,128)(2,1)S(1)}, f32[128,128]{1,0:T(8,128)S(1)}, bf16[128,256]{1,0:T(8,128)(2,1)S(1)}, s32[128,128]{1,0:T(8,128)S(1)}) custom-call(bf16[64,16,256]{2,1,0:T(8,128)(2,1)S(1)} %all-to-all-done.near_ref, s32[8,16]{1,0:T(8,128)} %bitcast.9, bf16[4,2048]{1,0:T(4,128)(2,1)} %state_w_hbm.1, ...), custom_call_target="tpu_custom_call" | custom-call | flops 268435456 | bytes 4194304 | tf_op jit(solution)/shard_map/pallas_call | solution.py:346
  32.6 0.0 collective-permute-done.3.far_ref
  32.6 16.1 %shard_map.86 = f32[128,128]{1,0:T(8,128)} custom-call(bf16[64,16,256]{2,1,0:T(8,128)(2,1)S(1)} %collective-permute-done.3.far_ref, f32[128,128]{1,0:T(8,128)S(1)} %bitcast.6, bf16[512,2048]{1,0:T(8,128)(2,1)S(1)} %get-tuple-element.26.hidden_w_ref, bf16[128,2048]{1,0:T(8,128)(2,1)S(1)} %get-tuple-element.27.in_w_ref, ...), custom_call_target="tpu_custom_call" | custom-call | tf_op jit(solution)/shard_map/pallas_call | solution.py:346
Async XLA Ops:
  1.7 24.1 %all-to-all-start = ((bf16[64,16,256]{2,1,0:T(8,128)(2,1)}), bf16[64,16,256]{2,1,0:T(8,128)(2,1)S(1)}, u32[]{:S(2)}, u32[]{:S(2)}) async-start(bf16[64,16,256]{2,1,0:T(8,128)(2,1)} %get-tuple-element.18), calls=%async_computation | async-start | bytes 1048576 | tf_op jit(solution)/shard_map/all_to_all | solution.py:396
  13.7 2.3 %collective-permute-start = (f32[2,8,128]{2,1,0:T(8,128)S(1)}, f32[2,8,128]{2,1,0:T(8,128)S(1)}, u32[]{:S(2)}, u32[]{:S(2)}) collective-permute-start(f32[2,8,128]{2,1,0:T(8,128)S(1)} %get-tuple-element.20), channel_id=1, source_target_pairs={{0,4},{4,0},{1,5},{5,1},{2,6},{6,2},{3,7},{7,3},{8,12},{12,8},{9,1... | collective-permute-start | bytes 24584 | tf_op jit(solution)/shard_map/ppermute | solution.py:392
  14.7 4.4 %collective-permute-start.1 = (f32[2,8,128]{2,1,0:T(8,128)S(1)}, f32[2,8,128]{2,1,0:T(8,128)S(1)}, u32[]{:S(2)}, u32[]{:S(2)}) collective-permute-start(f32[2,8,128]{2,1,0:T(8,128)S(1)} %get-tuple-element.21), channel_id=1, source_target_pairs={{4,8},{12,16},{20,24},{28,32},{36,40},{44,48},{52,56},{60,64},{68,... | collective-permute-start | bytes 24584 | tf_op jit(solution)/shard_map/ppermute | solution.py:395
  19.2 6.0 %collective-permute-start.2 = (f32[40,128]{1,0:T(8,128)S(1)}, f32[40,128]{1,0:T(8,128)S(1)}, u32[]{:S(2)}, u32[]{:S(2)}) collective-permute-start(f32[40,128]{1,0:T(8,128)S(1)} %get-tuple-element.22), channel_id=1, source_target_pairs={{0,1},{1,2},{2,3},{3,0},{4,5},{5,6},{6,7},{7,4},{8,9},{9,10},{10,1... | collective-permute-start | bytes 61448 | tf_op jit(solution)/shard_map/ppermute | solution.py:372
  25.8 6.8 %collective-permute-start.3 = (bf16[64,16,256]{2,1,0:T(8,128)(2,1)S(1)}, bf16[64,16,256]{2,1,0:T(8,128)(2,1)S(1)}, u32[]{:S(2)}, u32[]{:S(2)}) collective-permute-start(bf16[64,16,256]{2,1,0:T(8,128)(2,1)S(1)} %all-to-all-done.near_ref), channel_id=1, source_target_pairs={{0,4},{4,0},{1,5},{5,1},{2,6},{6,2},{3,7},{7,3},{8,12},{12,8},{9,1... | collective-permute-start | bytes 1572872 | tf_op jit(solution)/shard_map/ppermute | solution.py:408
  28.0 2.6 %collective-permute-start.4 = (f32[40,128]{1,0:T(8,128)S(1)}, f32[40,128]{1,0:T(8,128)S(1)}, u32[]{:S(2)}, u32[]{:S(2)}) collective-permute-start(f32[40,128]{1,0:T(8,128)S(1)} %get-tuple-element.25), channel_id=1, source_target_pairs={{1,0},{2,1},{3,2},{0,3},{5,4},{6,5},{7,6},{4,7},{9,8},{10,9},{11,1... | collective-permute-start | bytes 61448 | tf_op jit(solution)/shard_map/ppermute | solution.py:372
